TPU v7x, 512 devices: a whole 4x8x8 slice. The times are simulated.
512 devices in a mesh: blk: 512 (over z, y, x, core).
Axes of the slice: x: 4, y: 8, z: 8, core: 2. Of those that a mesh axis runs over, the one named last changes fastest.
Arguments:
- populations: float32 [16384, 19, 512], P('blk'), may hold values from 0 to 1, as said below
- coarse_faces: float32 [1024, 2, 19, 64], P('blk'), may hold values from 0 to 1, as said below
- neighbors: int32 [16384, 6], P('blk'), may hold values from -1 to 16383, as said below
- interface: int32 [16384, 2], P('blk'), may hold values from -1 to 1023, as said below
- solid: int32 [16384, 512], P('blk'), may hold values from 0 to 1, as said below
Outputs:
- advanced: float32 [16384, 19, 512], P('blk')
Inputs may be any that keep to these rules, and one draw needn't show every extreme that they name: `populations`: every entry is positive. `coarse_faces`: every entry is positive. `neighbors`: Symmetric: a is across face d of b exactly when b is across the opposite face of a. Blocks b with equal b // 32 share an owner. A block across a y or z face has the same owner; one across the +x (-x) face has the same owner or the next (previous) one. For each owner and each x direction at most 16 of its blocks have a neighbour with another owner, and some owner reaches 16 in each direction. The +y face of a block with interface[b, 0] >= 0 is -1 here. interface[b, 0] is owned by the next owner: interface[b, 0] // 2 == b // 32 + 1. interface[b, 1] is the quadrant, 0 to 3. Each pair of coarse block and quadrant appears at most once. `solid`: only cells with all three coordinates in 1..6 are wall cells.
All inputs are finite; a program needn't handle non-finite values.
Results may differ from a plain program's by a relative error of at most 0.0001.
Values sent between devices are 32-bit elements; how exact they have to be, the bound alone decides.
A program may use at most 64 MiB of HBM per device.

v0:
```python
import jax
import jax.numpy as jnp
import numpy as np
from jax import lax
from jax.sharding import PartitionSpec as P


def shifted(shard, axis, by):
    peers = lax.axis_size(axis)
    pairs = [(i, i + by) for i in range(peers) if 0 <= i + by < peers]
    return lax.ppermute(shard, axis, pairs)


def velocity_list():
    return [
        [0, 0, 0],
        [1, 0, 0],
        [-1, 0, 0],
        [0, 1, 0],
        [0, -1, 0],
        [0, 0, 1],
        [0, 0, -1],
        [1, 1, 0],
        [-1, -1, 0],
        [1, -1, 0],
        [-1, 1, 0],
        [1, 0, 1],
        [-1, 0, -1],
        [1, 0, -1],
        [-1, 0, 1],
        [0, 1, 1],
        [0, -1, -1],
        [0, 1, -1],
        [0, -1, 1],
    ]


def opposite_list():
    return [0, 2, 1, 4, 3, 6, 5, 8, 7, 10, 9, 12, 11, 14, 13, 16, 15, 18, 17]


def build_relax():
    velocity_set = np.array(velocity_list())
    shear_rate = 1.0 / 0.6
    vel_x = velocity_set[:, 0] * 1.0
    vel_y = velocity_set[:, 1] * 1.0
    vel_z = velocity_set[:, 2] * 1.0
    speed_sq = vel_x * vel_x + vel_y * vel_y + vel_z * vel_z
    moment_rows = [
        np.ones(19),
        19.0 * speed_sq - 30.0,
        (21.0 * speed_sq * speed_sq - 53.0 * speed_sq + 24.0) / 2.0,
        vel_x,
        (5.0 * speed_sq - 9.0) * vel_x,
        vel_y,
        (5.0 * speed_sq - 9.0) * vel_y,
        vel_z,
        (5.0 * speed_sq - 9.0) * vel_z,
        3.0 * vel_x * vel_x - speed_sq,
        (3.0 * speed_sq - 5.0) * (3.0 * vel_x * vel_x - speed_sq),
        vel_y * vel_y - vel_z * vel_z,
        (3.0 * speed_sq - 5.0) * (vel_y * vel_y - vel_z * vel_z),
        vel_x * vel_y,
        vel_y * vel_z,
        vel_x * vel_z,
        (vel_y * vel_y - vel_z * vel_z) * vel_x,
        (vel_z * vel_z - vel_x * vel_x) * vel_y,
        (vel_x * vel_x - vel_y * vel_y) * vel_z,
    ]
    moments = np.stack(moment_rows)
    relax_rates = np.array(
        [
            0.0,
            1.19,
            1.4,
            0.0,
            1.2,
            0.0,
            1.2,
            0.0,
            1.2,
            shear_rate,
            1.4,
            shear_rate,
            1.4,
            shear_rate,
            shear_rate,
            shear_rate,
            1.98,
            1.98,
            1.98,
        ]
    )
    row_norms = np.sum(moments * moments, axis=1)
    return moments.T @ ((relax_rates / row_norms)[:, None] * moments)


def build_crossing():
    velocity_set = velocity_list()
    crossing_list = []
    for face_dir in range(6):
        axis_pos = face_dir // 2
        sign_val = 1 if face_dir % 2 == 0 else -1
        members = [
            lattice_dir
            for lattice_dir in range(19)
            if velocity_set[lattice_dir][axis_pos] == -sign_val
        ]
        crossing_list.append(members)
    return crossing_list


def build_layers():
    layer_list = []
    for face_dir in range(6):
        axis_pos = face_dir // 2
        level = 7 if face_dir % 2 == 0 else 0
        others = [other_axis for other_axis in range(3) if other_axis != axis_pos]
        cell_list = []
        for first_coord in range(8):
            for second_coord in range(8):
                coords = [0, 0, 0]
                coords[axis_pos] = level
                coords[others[0]] = first_coord
                coords[others[1]] = second_coord
                cell_list.append(64 * coords[0] + 8 * coords[1] + coords[2])
        layer_list.append(np.array(cell_list, dtype=np.int32))
    return layer_list


def build_sources():
    velocity_set = velocity_list()
    side_table = np.full((19, 512), -1, dtype=np.int32)
    ghost_table = np.zeros((19, 512), dtype=np.int32)
    for lattice_dir in range(19):
        for cell in range(512):
            coords = [cell // 64, cell // 8 % 8, cell % 8]
            source = [
                coords[axis_pos] - velocity_set[lattice_dir][axis_pos] for axis_pos in range(3)
            ]
            outside = [
                axis_pos for axis_pos in range(3) if source[axis_pos] < 0 or source[axis_pos] > 7
            ]
            if len(outside) == 1:
                axis_pos = outside[0]
                side_table[lattice_dir, cell] = 2 * axis_pos + (0 if source[axis_pos] > 7 else 1)
                others = [other_axis for other_axis in range(3) if other_axis != axis_pos]
                ghost_table[lattice_dir, cell] = 8 * source[others[0]] + source[others[1]]
            elif len(outside) > 1:
                side_table[lattice_dir, cell] = 6
    return (side_table, ghost_table)


def build_quadrants():
    quad_cells = np.zeros((4, 64), dtype=np.int32)
    for quad in range(4):
        for fine_i in range(8):
            for fine_k in range(8):
                quad_cells[quad, 8 * fine_i + fine_k] = (
                    8 * (4 * (quad // 2) + fine_i // 2) + 4 * (quad % 2) + fine_k // 2
                )
    return quad_cells


def build_offsets():
    velocity_set = velocity_list()
    return [
        int(
            64 * velocity_set[lattice_dir][0]
            + 8 * velocity_set[lattice_dir][1]
            + velocity_set[lattice_dir][2]
        )
        for lattice_dir in range(19)
    ]


def equilibrium(states):
    velocity_f32 = jnp.asarray(np.array(velocity_list()), dtype=jnp.float32)
    weight_f32 = jnp.asarray(
        np.array([1.0 / 3.0] + [1.0 / 18.0] * 6 + [1.0 / 36.0] * 12), dtype=jnp.float32
    )
    density = jnp.sum(states, axis=1)
    momentum = jnp.einsum("qa,mqn->man", velocity_f32, states, precision=lax.Precision.HIGHEST)
    velocity = momentum / density[:, None, :]
    project = jnp.einsum("qa,man->mqn", velocity_f32, velocity, precision=lax.Precision.HIGHEST)
    square = jnp.sum(velocity * velocity, axis=1)
    return (
        weight_f32[None, :, None]
        * density[:, None, :]
        * (1.0 + 3.0 * project + 4.5 * project * project - 1.5 * square[:, None, :])
    )


def collide(states):
    relax_matrix = jnp.asarray(build_relax(), dtype=jnp.float32)
    balance = equilibrium(states)
    return states - jnp.einsum(
        "pq,mqn->mpn", relax_matrix, states - balance, precision=lax.Precision.HIGHEST
    )


def layer_of(relaxed, face_dir):
    crossing_sets = build_crossing()
    layer_cells = build_layers()
    picked = jnp.take(relaxed, jnp.asarray(crossing_sets[face_dir], dtype=jnp.int32), axis=1)
    picked = jnp.take(picked, jnp.asarray(layer_cells[face_dir ^ 1], dtype=jnp.int32), axis=2)
    return picked.reshape(relaxed.shape[0], 320)


def interface_values(coarse_tiles):
    crossing_sets = build_crossing()
    coarse_ratio = 0.6 / 1.1
    total = coarse_tiles.shape[0]
    outputs = []
    for time_frac in (0.0, 0.5):
        blended = (1.0 - time_frac) * coarse_tiles[:, 0] + time_frac * coarse_tiles[:, 1]
        balance = equilibrium(blended)
        ghost_vals = balance + coarse_ratio * (blended - balance)
        chosen = jnp.take(ghost_vals, jnp.asarray(crossing_sets[2], dtype=jnp.int32), axis=1)
        outputs.append(chosen.reshape(total, 320))
    return jnp.stack(outputs, axis=1)


def spread_quadrant(picked, quadrant):
    quad_table = jnp.asarray(build_quadrants(), dtype=jnp.int32)
    total = picked.shape[0]
    ghost_view = picked.reshape(total, 2, 5, 64)
    cell_index = jnp.take(quad_table, quadrant, axis=0)
    cell_index = jnp.broadcast_to(cell_index[:, None, None, :], (total, 2, 5, 64))
    return jnp.take_along_axis(ghost_view, cell_index, axis=3).reshape(total, 2, 320)


def stream(relaxed, initial, ghosts, present, solid):
    crossing_sets = build_crossing()
    source_side, ghost_cell = build_sources()
    shift_offsets = build_offsets()
    opposite_dir = opposite_list()
    total = relaxed.shape[0]
    fluid = solid == 0
    ghost_view = ghosts.reshape(total, 6, 5, 64)
    pulled = []
    for lattice_dir in range(19):
        moved = jnp.roll(relaxed[:, lattice_dir], shift_offsets[lattice_dir], axis=1)
        usable = jnp.roll(fluid, shift_offsets[lattice_dir], axis=1)
        for face_dir in range(6):
            if lattice_dir in crossing_sets[face_dir]:
                slot_pos = crossing_sets[face_dir].index(lattice_dir)
                through = jnp.asarray(source_side[lattice_dir] == face_dir)[None, :]
                fetched = jnp.take(
                    ghost_view[:, face_dir, slot_pos], jnp.asarray(ghost_cell[lattice_dir]), axis=1
                )
                moved = jnp.where(through, fetched, moved)
                usable = jnp.where(through, present[:, face_dir : face_dir + 1], usable)
        edge_mask = jnp.asarray(source_side[lattice_dir] == 6)[None, :]
        usable = jnp.where(edge_mask, False, usable)
        pulled.append(jnp.where(usable, moved, relaxed[:, opposite_dir[lattice_dir]]))
    read = jnp.stack(pulled, axis=1)
    return jnp.where(fluid[:, None, :], read, initial)


def remote_faces(layers, neighbors, first_block, block_count):
    below_index = jnp.clip(neighbors[:, 1] - (first_block - block_count), 0, block_count - 1)
    above_index = jnp.clip(neighbors[:, 0] - (first_block + block_count), 0, block_count - 1)
    from_below = shifted(layers[:, 1], "blk", 1)
    from_above = shifted(layers[:, 0], "blk", -1)
    lower_ghost = jnp.take(from_below, below_index, axis=0)
    upper_ghost = jnp.take(from_above, above_index, axis=0)
    return (lower_ghost, upper_ghost)


def body(populations, coarse_faces, neighbors, interface, solid):
    block_count = populations.shape[0]
    coarse_count = coarse_faces.shape[0]
    position = lax.axis_index("blk")
    first_block = position * block_count
    received = shifted(coarse_faces, "blk", -1)
    coarse_vals = interface_values(received)
    coarse_local = jnp.clip(interface[:, 0] - (position + 1) * coarse_count, 0, coarse_count - 1)
    has_coarse = interface[:, 0] >= 0
    picked = jnp.take(coarse_vals, coarse_local, axis=0)
    fine_ghost = spread_quadrant(picked, interface[:, 1])
    face_ids = jnp.arange(6, dtype=jnp.int32)
    present = (neighbors >= 0) | (face_ids[None, :] == 2) & has_coarse[:, None]
    local_index = neighbors - first_block
    is_local = (local_index >= 0) & (local_index < block_count)
    local_clip = jnp.clip(local_index, 0, block_count - 1)
    current = populations
    for substep in range(2):
        relaxed = collide(current)
        layers = jnp.stack([layer_of(relaxed, face_dir) for face_dir in range(6)], axis=1)
        lower_ghost, upper_ghost = remote_faces(layers, neighbors, first_block, block_count)
        ghosts = []
        for face_dir in range(6):
            fetched = jnp.take(layers[:, face_dir], local_clip[:, face_dir], axis=0)
            if face_dir == 0:
                fetched = jnp.where(is_local[:, 0:1], fetched, upper_ghost)
            if face_dir == 1:
                fetched = jnp.where(is_local[:, 1:2], fetched, lower_ghost)
            if face_dir == 2:
                fetched = jnp.where(has_coarse[:, None], fine_ghost[:, substep], fetched)
            ghosts.append(fetched)
        current = stream(relaxed, populations, jnp.stack(ghosts, axis=1), present, solid)
    return current


def solution(mesh):
    placed = (
        P("blk", None, None),
        P("blk", None, None, None),
        P("blk", None),
        P("blk", None),
        P("blk", None),
    )
    return jax.shard_map(
        body, mesh=mesh, in_specs=placed, out_specs=P("blk", None, None), check_vma=False
    )
```

profile of v0, /device:TPU:255, one launch (start us, length us, event | category | flops | bytes accessed | tf_op | source)
XLA Modules:
  0.0 522.7 jit_solution(15400187523703013417)
XLA Ops:
  5.9 2.3 fusion.4
  9.7 1.9 copy.531
  12.3 2.2 gather_fusion.4
  14.7 4.9 collective-permute-start
  22.8 2.2 gather_fusion.9
  28.0 2.2 collective-permute-start.2
  46.7 2.0 copy.539
  48.8 2.2 gather_fusion.14
  55.1 2.0 copy.556
  57.2 2.2 gather_fusion.24
  61.1 2.0 copy.560
  63.7 2.9 gather_fusion.28
  94.6 3.0 copy.552
  97.6 2.2 gather_fusion.20
  134.3 156.5 %gather_fusion.2 = f32[20480]{0:T(1024)S(1)} fusion(f32[32,2,5,64]{3,2,0,1:T(8,128)S(1)} %broadcast_select_fusion.2, s32[20480]{0:T(1024)S(1)} %reshape.1060), kind=kCustom, calls=%fused_computation.104 | custom fusion | bytes 491520 | tf_op jit(solution)/shard_map/jit(take_along_axis)/gather | solution.py:230
  322.8 12.3 %gather_fusion.38 = f32[512,32]{1,0:T(8,128)S(1)} fusion(f32[32,64]{0,1:T(8,128)S(1)} %get-tuple-element.142, s32[1024]{0:T(1024)} %get-tuple-element.230), kind=kCustom, calls=%fused_computation.54.clone | custom fusion | bytes 133120 | tf_op jit(solution)/shard_map/jit(_take)/gather | solution.py:249
  357.2 2.2 multiply_reduce_fusion
  362.0 2.3 fusion
  372.8 3.0 copy.620
  375.8 3.0 gather_fusion.61
  383.7 3.0 copy.616
  386.7 3.0 gather_fusion.56
  390.9 9.1 %collective-permute-start.3 = (f32[32,320]{1,0:T(8,128)S(1)}, f32[32,320]{1,0:T(8,128)S(1)}, u32[]{:S(2)}, u32[]{:S(2)}) collective-permute-start(f32[32,320]{1,0:T(8,128)S(1)} %squeeze_stack_reshape.46), channel_id=1, source_target_pairs={{0,1},{1,2},{2,3},{3,4},{4,5},{5,6},{6,7},{7,8},{8,9},{9,10},{10,1... | collective-permute-start | bytes 122888 | tf_op jit(solution)/shard_map/ppermute | solution.py:11
  399.9 2.0 copy.624
  401.9 2.3 gather_fusion.66
  405.5 2.0 copy.628
  407.5 2.3 gather_fusion.70
  411.0 3.0 copy.632
  414.0 2.3 gather_fusion.74
  419.1 3.0 copy.636
  422.1 3.0 gather_fusion.78
  519.7 2.6 broadcast_select_fusion
  (869 shorter events, 267.8 us)
Async XLA Ops:
  14.7 285.5 %collective-permute-start = (f32[32,320]{1,0:T(8,128)S(1)}, f32[32,320]{1,0:T(8,128)S(1)}, u32[]{:S(2)}, u32[]{:S(2)}) collective-permute-start(f32[32,320]{1,0:T(8,128)S(1)} %squeeze_stack_reshape.40), channel_id=1, source_target_pairs={{0,1},{1,2},{2,3},{3,4},{4,5},{5,6},{6,7},{7,8},{8,9},{9,10},{10,1... | collective-permute-start | bytes 122888 | tf_op jit(solution)/shard_map/ppermute | solution.py:11
  19.7 26.5 %copy-start.151 = (s32[1024]{0:T(1024)}, s32[1024]{0:T(1024)S(1)}, u32[]{:S(2)}) copy-start(s32[1024]{0:T(1024)S(1)} %get-tuple-element.220) | copy-start | bytes 12292
  22.8 20.8 %copy-start.131 = (s32[32,6]{0,1:T(8,128)S(1)}, s32[32,6]{0,1:T(8,128)}, u32[]{:S(2)}) copy-start(s32[32,6]{0,1:T(8,128)} %param.210) | copy-start | bytes 2308
  22.8 21.4 %copy-start.219 = (s32[32,2]{0,1:T(2,128)S(1)}, s32[32,2]{0,1:T(2,128)}, u32[]{:S(2)}) copy-start(s32[32,2]{0,1:T(2,128)} %param.211) | copy-start | bytes 772
  25.5 278.5 %collective-permute-start.1 = (f32[32,320]{1,0:T(8,128)S(1)}, f32[32,320]{1,0:T(8,128)S(1)}, u32[]{:S(2)}, u32[]{:S(2)}) collective-permute-start(f32[32,320]{1,0:T(8,128)S(1)} %squeeze_stack_reshape.41), channel_id=1, source_target_pairs={{1,0},{2,1},{3,2},{4,3},{5,4},{6,5},{7,6},{8,7},{9,8},{10,9},{11,1... | collective-permute-start | bytes 122888 | tf_op jit(solution)/shard_map/ppermute | solution.py:11
  28.0 99.0 %collective-permute-start.2 = (f32[2,2,19,64]{3,2,0,1:T(8,128)}, f32[2,2,19,64]{3,2,0,1:T(8,128)}, u32[]{:S(2)}, u32[]{:S(2)}) collective-permute-start(f32[2,2,19,64]{3,2,0,1:T(8,128)} %copy.543), channel_id=1, source_target_pairs={{1,0},{2,1},{3,2},{4,3},{5,4},{6,5},{7,6},{8,7},{9,8},{10,9},{11,1... | collective-permute-start | bytes 58376 | tf_op jit(solution)/shard_map/ppermute | solution.py:11
  35.5 31.1 %copy-start.203 = (pred[64]{0:T(512)(128)(4,1)}, pred[64]{0:T(512)(128)(4,1)S(1)}, u32[]{:S(2)}) copy-start(pred[64]{0:T(512)(128)(4,1)S(1)} %compare_and_fusion.2) | copy-start | bytes 196
  44.3 15.9 %copy-start.170 = (pred[32]{0:T(512)(128)(4,1)}, pred[32]{0:T(512)(128)(4,1)S(1)}, u32[]{:S(2)}) copy-start(pred[32]{0:T(512)(128)(4,1)S(1)} %get-tuple-element.186) | copy-start | bytes 100
  44.3 26.4 %copy-start.168 = (pred[32]{0:T(512)(128)(4,1)}, pred[32]{0:T(512)(128)(4,1)S(1)}, u32[]{:S(2)}) copy-start(pred[32]{0:T(512)(128)(4,1)S(1)} %get-tuple-element.14) | copy-start | bytes 100
  69.5 18.3 %copy-start.135 = (s32[1024]{0:T(1024)S(1)}, s32[1024]{0:T(1024)}, u32[]{:S(2)}) copy-start(s32[1024]{0:T(1024)} %get-tuple-element.245) | copy-start | bytes 12292
  72.7 16.7 %copy-start.163 = (s32[1024]{0:T(1024)}, s32[1024]{0:T(1024)S(1)}, u32[]{:S(2)}) copy-start(s32[1024]{0:T(1024)S(1)} %get-tuple-element.251) | copy-start | bytes 12292
  73.3 24.3 %copy-start.158 = (s32[1024]{0:T(1024)}, s32[1024]{0:T(1024)S(1)}, u32[]{:S(2)}) copy-start(s32[1024]{0:T(1024)S(1)} %get-tuple-element.242) | copy-start | bytes 12292
  73.3 17.9 %copy-start.45 = (s32[32,64]{1,0:T(8,128)S(1)}, s32[32,64]{1,0:T(8,128)}, u32[]{:S(2)}) copy-start(s32[32,64]{1,0:T(8,128)} %broadcast_add_fusion) | copy-start | bytes 24580
  134.2 156.7 %copy-start.40 = (s32[32,320]{1,0:T(8,128)S(1)}, s32[32,320]{1,0:T(8,128)}, u32[]{:S(2)}) copy-start(s32[32,320]{1,0:T(8,128)} %broadcast_in_dim.1214) | copy-start | bytes 122884
  134.2 156.7 %copy-start.41 = (s32[32,320]{1,0:T(8,128)S(1)}, s32[32,320]{1,0:T(8,128)}, u32[]{:S(2)}) copy-start(s32[32,320]{1,0:T(8,128)} %broadcast_in_dim.1217) | copy-start | bytes 122884
  134.2 156.7 %copy-start.90 = (pred[32,320]{1,0:T(8,128)(4,1)S(1)}, pred[32,320]{1,0:T(8,128)(4,1)}, u32[]{:S(2)}) copy-start(pred[32,320]{1,0:T(8,128)(4,1)} %broadcast_in_dim.1211) | copy-start | bytes 30724
  134.3 157.4 %copy-start.143 = (pred[32]{0:T(512)(128)(4,1)S(1)}, pred[32]{0:T(512)(128)(4,1)}, u32[]{:S(2)}) copy-start(pred[32]{0:T(512)(128)(4,1)} %copy-done.142) | copy-start | bytes 100
  134.3 157.4 %copy-start.172 = (pred[32]{0:T(512)(128)(4,1)S(1)}, pred[32]{0:T(512)(128)(4,1)}, u32[]{:S(2)}) copy-start(pred[32]{0:T(512)(128)(4,1)} %get-tuple-element.188) | copy-start | bytes 100
  134.3 157.6 %copy-start.139 = (s32[1024]{0:T(1024)S(1)}, s32[1024]{0:T(1024)}, u32[]{:S(2)}) copy-start(s32[1024]{0:T(1024)} %get-tuple-element.240) | copy-start | bytes 12292
  321.1 15.5 %copy-start.31 = (f32[512,32]{0,1:T(8,128)S(1)}, f32[512,32]{0,1:T(8,128)}, u32[]{:S(2)}) copy-start(f32[512,32]{0,1:T(8,128)} %copy.577) | copy-start | bytes 196612
  321.1 15.5 %copy-start.57 = (pred[32,456]{1,0:T(8,128)(4,1)S(1)}, pred[32,456]{1,0:T(8,128)(4,1)}, u32[]{:S(2)}) copy-start(pred[32,456]{1,0:T(8,128)(4,1)} %get-tuple-element.166) | copy-start | bytes 43780
  321.1 15.5 %copy-start.78 = (pred[32]{0:T(512)(128)(4,1)S(1)}, pred[32]{0:T(512)(128)(4,1)}, u32[]{:S(2)}) copy-start(pred[32]{0:T(512)(128)(4,1)} %get-tuple-element.204) | copy-start | bytes 100
  321.1 15.5 %copy-start.83 = (pred[32]{0:T(512)(128)(4,1)S(1)}, pred[32]{0:T(512)(128)(4,1)}, u32[]{:S(2)}) copy-start(pred[32]{0:T(512)(128)(4,1)} %get-tuple-element.203) | copy-start | bytes 100
  321.2 15.5 %copy-start.127 = (pred[32,56]{1,0:T(8,128)(4,1)S(1)}, pred[32,56]{1,0:T(8,128)(4,1)}, u32[]{:S(2)}) copy-start(pred[32,56]{1,0:T(8,128)(4,1)} %get-tuple-element.168) | copy-start | bytes 5380
  321.2 15.5 %copy-start.197 = (pred[512]{0:T(512)(128)(4,1)S(1)}, pred[512]{0:T(512)(128)(4,1)}, u32[]{:S(2)}) copy-start(pred[512]{0:T(512)(128)(4,1)} %constant.329.clone) | copy-start | bytes 1540
  321.2 15.5 %copy-start.198 = (pred[512]{0:T(512)(128)(4,1)S(1)}, pred[512]{0:T(512)(128)(4,1)}, u32[]{:S(2)}) copy-start(pred[512]{0:T(512)(128)(4,1)} %constant.331.clone) | copy-start | bytes 1540
  321.2 15.5 %copy-start.199 = (pred[512]{0:T(512)(128)(4,1)S(1)}, pred[512]{0:T(512)(128)(4,1)}, u32[]{:S(2)}) copy-start(pred[512]{0:T(512)(128)(4,1)} %constant.332.clone) | copy-start | bytes 1540
  322.7 14.8 %copy-start.9 = (f32[512,32]{0,1:T(8,128)S(1)}, f32[512,32]{0,1:T(8,128)}, u32[]{:S(2)}) copy-start(f32[512,32]{0,1:T(8,128)} %copy.581) | copy-start | bytes 196612
  322.7 14.8 %copy-start.56 = (pred[32,447]{1,0:T(8,128)(4,1)S(1)}, pred[32,447]{1,0:T(8,128)(4,1)}, u32[]{:S(2)}) copy-start(pred[32,447]{1,0:T(8,128)(4,1)} %get-tuple-element.163) | copy-start | bytes 42916
  322.7 14.8 %copy-start.80 = (pred[32]{0:T(512)(128)(4,1)S(1)}, pred[32]{0:T(512)(128)(4,1)}, u32[]{:S(2)}) copy-start(pred[32]{0:T(512)(128)(4,1)} %get-tuple-element.201) | copy-start | bytes 100
  381.8 96.0 %collective-permute-start.4 = (f32[32,320]{1,0:T(8,128)S(1)}, f32[32,320]{1,0:T(8,128)S(1)}, u32[]{:S(2)}, u32[]{:S(2)}) collective-permute-start(f32[32,320]{1,0:T(8,128)S(1)} %squeeze_stack_reshape.47), channel_id=1, source_target_pairs={{1,0},{2,1},{3,2},{4,3},{5,4},{6,5},{7,6},{8,7},{9,8},{10,9},{11,1... | collective-permute-start | bytes 122888 | tf_op jit(solution)/shard_map/ppermute | solution.py:11
  390.9 82.5 %collective-permute-start.3 = (f32[32,320]{1,0:T(8,128)S(1)}, f32[32,320]{1,0:T(8,128)S(1)}, u32[]{:S(2)}, u32[]{:S(2)}) collective-permute-start(f32[32,320]{1,0:T(8,128)S(1)} %squeeze_stack_reshape.46), channel_id=1, source_target_pairs={{0,1},{1,2},{2,3},{3,4},{4,5},{5,6},{6,7},{7,8},{8,9},{9,10},{10,1... | collective-permute-start | bytes 122888 | tf_op jit(solution)/shard_map/ppermute | solution.py:11
  (203 other events, 1042.3 us)
where the time goes:
time: 533 us; the launch traced here: 523 us
  local copies, waits for them, and re-layouts  399 us (75%)
  other arithmetic  84.3 us (16%)
  starting transfers between devices  19.9 us (4%)
  matrix products  15.3 us (3%)
    gather x3, local copies, waits for them, and re-layouts, spread_quadrant(): jnp.take_along_axis(ghost_view, cell_index, axis=3).reshape(total, 2, 320)  157 us
    gather x120, local copies, waits for them, and re-layouts, stream(): jnp.take(ghost_view[:, face_dir, slot_pos], jnp.asarray(ghost_cell[lattic...  112 us
    gather x24, local copies, waits for them, and re-layouts, layer_of(): jnp.take(relaxed, jnp.asarray(crossing_sets[face_dir], dtype=jnp.int32),...  40 us
    gather x20, local copies, waits for them, and re-layouts, layer_of(): jnp.take(picked, jnp.asarray(layer_cells[face_dir ^ 1], dtype=jnp.int32),...  33.3 us
    unnamed x16, other arithmetic  22.7 us
    squeeze x16, other arithmetic, stream(): relaxed[:, lattice_dir]  21.4 us
    ppermute x5, starting transfers between devices, shifted(): return lax.ppermute(shard, axis, pairs)  19.9 us
    gather x20, other arithmetic  13.9 us
  transfers between devices with their start and end apart: 5, of which 0 were waited for; matrix products, arithmetic and copies ran while one was open for 69% of the time, Pallas kernels for 0%

commit v1 on v0

v1 whole, which is shorter than its diff:
```python
import functools

import jax
import jax.numpy as jnp
import numpy as np
from jax import lax
from jax.experimental import pallas as pl
from jax.experimental.pallas import tpu as pltpu
from jax.sharding import PartitionSpec as P

MESH = pl.DeviceIdType.MESH
F32 = jnp.float32
BF16 = jnp.bfloat16
I32 = jnp.int32

VEL = [
    (0, 0, 0),
    (1, 0, 0),
    (-1, 0, 0),
    (0, 1, 0),
    (0, -1, 0),
    (0, 0, 1),
    (0, 0, -1),
    (1, 1, 0),
    (-1, -1, 0),
    (1, -1, 0),
    (-1, 1, 0),
    (1, 0, 1),
    (-1, 0, -1),
    (1, 0, -1),
    (-1, 0, 1),
    (0, 1, 1),
    (0, -1, -1),
    (0, 1, -1),
    (0, -1, 1),
]
OPP = [VEL.index((-x, -y, -z)) for x, y, z in VEL]
CROSS = [
    [q for q in range(19) if VEL[q][d // 2] == (-1 if d % 2 == 0 else 1)] for d in range(6)
]
BIT = [9 * (x + 1) + 3 * (y + 1) + (z + 1) for x, y, z in VEL]
BLK = 32
TILE = 128
ROWS = 8


def relax_delta(f):
    s = 1.0 / 0.6
    sx, dx = f[1] + f[2], f[1] - f[2]
    sy, dy = f[3] + f[4], f[3] - f[4]
    sz, dz = f[5] + f[6], f[5] - f[6]
    s7, d7 = f[7] + f[8], f[7] - f[8]
    s9, d9 = f[9] + f[10], f[9] - f[10]
    s11, d11 = f[11] + f[12], f[11] - f[12]
    s13, d13 = f[13] + f[14], f[13] - f[14]
    s15, d15 = f[15] + f[16], f[15] - f[16]
    s17, d17 = f[17] + f[18], f[17] - f[18]
    sa, ta = s7 + s9, s7 - s9
    sb, tb = s11 + s13, s11 - s13
    sc, tc = s15 + s17, s15 - s17
    ax, ay = d7 + d9, d7 - d9
    bx, bz = d11 + d13, d11 - d13
    cy, cz = d15 + d17, d15 - d17
    x2, mx = ax + bx, ax - bx
    y2, my = ay + cy, cy - ay
    z2, mz = bz + cz, bz - cz
    jx, jy, jz = dx + x2, dy + y2, dz + z2
    ab = sa + sb
    s2 = ab + sc
    yz = sy + sz
    s1 = sx + yz
    rho = f[0] + (s1 + s2)
    inv = 1.0 / rho
    ux, uy, uz = jx * inv, jy * inv, jz * inv
    xx, yy, zz = jx * ux, jy * uy, jz * uz
    jj = (xx + yy) + zz
    m1 = (s2 - f[0]) - jj
    m2 = 9.0 * f[0] - 7.0 * s1 - 2.0 * s2 + 5.5 * jj
    c1 = m1 * (19.0 * 1.19 / 2394.0)
    c2 = m2 * (1.4 / 252.0)
    a9 = (sx + sx) - yz
    b9 = ab - (sc + sc)
    e9 = (xx + xx) - (yy + zz)
    c9 = (a9 + b9 - e9) * (s / 36.0)
    c10 = (b9 - 2.0 * a9 + 0.5 * e9) * (1.4 / 72.0)
    a11 = sy - sz
    b11 = sa - sb
    e11 = yy - zz
    c11 = (a11 + b11 - e11) * (s / 12.0)
    c12 = (b11 - 2.0 * a11 + 0.5 * e11) * (1.4 / 24.0)
    c13 = (ta - jx * uy) * (s / 4.0)
    c14 = (tc - jy * uz) * (s / 4.0)
    c15 = (tb - jx * uz) * (s / 4.0)
    g = (5.0 / 3.0) * 1.2 / 40.0
    c4 = (x2 - 2.0 * dx) * g
    c6 = (y2 - 2.0 * dy) * g
    c8 = (z2 - 2.0 * dz) * g
    h = 1.98 / 8.0
    c16, c17, c18 = mx * h, my * h, mz * h
    r0 = 12.0 * c2 - 30.0 * c1
    ra = -11.0 * c1 - 4.0 * c2
    rd = 8.0 * c1 + c2
    p9 = c9 - 2.0 * c10
    p11 = c11 - 2.0 * c12
    n9 = c9 + c10
    n11 = c11 + c12
    ex = ra + 2.0 * p9
    et = ra - p9
    ey, ez = et + p11, et - p11
    rt = rd + n9
    exy, exz = rt + n11, rt - n11
    eyz = rd - 2.0 * n9
    ox, oy, oz = -4.0 * c4, -4.0 * c6, -4.0 * c8
    xa, ya = c4 + c16, c6 - c17
    xb, zb = c4 - c16, c8 + c18
    yc, zc = c6 + c17, c8 - c18
    e7, e9_ = exy + c13, exy - c13
    e11_, e13 = exz + c15, exz - c15
    e15, e17 = eyz + c14, eyz - c14
    o7, o9 = xa + ya, xa - ya
    o11, o13 = xb + zb, xb - zb
    o15, o17 = yc + zc, yc - zc
    out = [f[0] - r0]
    for q, even, odd in (
        (1, ex, ox),
        (3, ey, oy),
        (5, ez, oz),
        (7, e7, o7),
        (9, e9_, o9),
        (11, e11_, o11),
        (13, e13, o13),
        (15, e15, o15),
        (17, e17, o17),
    ):
        out.append(f[q] - (even + odd))
        out.append(f[q + 1] - (even - odd))
    return out


def split(x):
    hi = x.astype(BF16)
    lo = (x - hi.astype(F32)).astype(BF16)
    return jnp.concatenate([hi, lo], axis=0)


def roll(x, by):
    by %= TILE
    return pltpu.roll(x, by, 1) if by else x


def lanes():
    return lax.broadcasted_iota(I32, (ROWS, TILE), 1)


def face_lanes(d, t, lane):
    if d == 0:
        return lane >= 64 if t == 3 else None
    if d == 1:
        return lane < 64 if t == 0 else None
    pos = ((lane >> 3) & 7) if d < 4 else (lane & 7)
    return pos == (7 if d % 2 == 0 else 0)


def cols(t):
    return pl.ds(t * TILE, TILE)


def rows_of(r):
    return pl.ds(pl.multiple_of(r * ROWS, ROWS), ROWS)


def store_post(post, ref, packs, xs, rows, t, lane):
    for q in range(19):
        ref[q, rows, cols(t)] = post[q]
    high = lane & 7
    mid = (lane >> 3) & 7
    for d in range(2, 6):
        acc = post[CROSS[d][0]]
        for s in range(1, 5):
            step = (8 if d < 4 else 1) * s
            pos = mid if d < 4 else high
            by, at = (step, s) if d % 2 == 0 else (-step, 7 - s)
            acc = jnp.where(pos == at, roll(post[CROSS[d][s]], by), acc)
        packs[d - 2, rows, cols(t)] = acc
    if t in (0, 3):
        d = 0 if t == 0 else 1
        keep = lane < 64 if t == 0 else lane >= 64
        for s in range(2):
            a, b = CROSS[d][2 * s], CROSS[d][2 * s + 1]
            xs[d, rows, cols(s)] = jnp.where(keep, post[a], roll(post[b], 64))
        xs[d, rows, cols(2)] = post[CROSS[d][4]]


def stream(ref, gh, gx, code_ref, rows, t, lane):
    post = [ref[q, rows, cols(t)] for q in range(19)]
    code = code_ref[rows, cols(t)]
    upper = lane >= 64

    def merged(ex, here, load, edge):
        if ex == 0:
            return here
        near = t - ex
        if 0 <= near <= 3:
            other = load(near)
        else:
            other = edge
        if other is None:
            return here
        return jnp.where(upper, other, here) if ex == 1 else jnp.where(upper, here, other)

    out = [post[0]]
    for q in range(1, 19):
        ex, ey, ez = VEL[q]
        edge = None
        if ex != 0 and not 0 <= t - ex <= 3:
            d = 0 if ex == -1 else 1
            n = CROSS[d].index(q)
            edge = gx[d, rows, cols(n // 2)]
            if n % 2:
                edge = roll(edge, 64)
        base = 64 * ex
        src = merged(ex, post[q], lambda u: ref[q, rows, cols(u)], edge)
        moved = roll(src, base + 8 * ey + ez)
        for d, comp in ((2 if ey < 0 else 3, ey), (4 if ez < 0 else 5, ez)):
            if comp == 0:
                continue
            s = CROSS[d].index(q)
            if d < 4:
                off = (56 - 8 * s) * (1 if d == 2 else -1) + base + ez
            else:
                off = (7 - s) * (1 if d == 4 else -1) + base + 8 * ey
            g = merged(
                ex, gh[d - 2, rows, cols(t)], lambda u: gh[d - 2, rows, cols(u)], None
            )
            moved = jnp.where(face_lanes(d, t, lane), roll(g, off), moved)
        usable = (code & (1 << BIT[q])) != 0
        out.append(jnp.where(usable, moved, post[OPP[q]]))
    return out


def kernel(
    n,
    pops,
    coarse,
    nbr,
    itf,
    solid,
    out,
    f,
    pa,
    pb,
    ov,
    packs,
    gh,
    gxl,
    gx,
    xs,
    xr,
    cfv,
    nv,
    iv,
    sv,
    cs,
    cr,
    gc,
    code,
    pw,
    pyz,
    pxl,
    pxr,
    pc,
    in_sem,
    out_sem,
    send_sem,
    recv_sem,
):
    me = lax.axis_index("blk")
    nxt = lax.rem(me + 1, n)
    prv = lax.rem(me + n - 1, n)

    barrier = pltpu.get_barrier_semaphore()
    for peer in (prv, nxt):
        pl.semaphore_signal(barrier, inc=1, device_id=(peer,), device_id_type=MESH)

    def fetch(k, src, dst):
        c = pltpu.make_async_copy(src, dst, in_sem.at[k])
        c.start()
        return c

    def tile_of(ref, t, w=1):
        return ref.at[:, :, pl.ds(t * TILE, w * TILE)]

    in3 = fetch(0, tile_of(pops, 3), tile_of(f, 3))
    in0 = fetch(1, tile_of(pops, 0), tile_of(f, 0))
    inc = fetch(2, coarse, cfv)
    inn = fetch(3, nbr, nv)
    ini = fetch(4, itf, iv)
    ins = fetch(5, solid, sv)
    in12 = fetch(6, tile_of(pops, 1, 2), tile_of(f, 1, 2))

    def send(k, src, dst, peer):
        c = pltpu.make_async_remote_copy(
            src_ref=src,
            dst_ref=dst,
            send_sem=send_sem.at[k],
            recv_sem=recv_sem.at[k],
            device_id=(peer,),
            device_id_type=MESH,
        )
        c.start()
        return c

    lane = lanes()

    def first_collide(t):
        def step(r, carry):
            rows = rows_of(r)
            post = relax_delta([f[q, rows, cols(t)] for q in range(19)])
            store_post(post, pa, packs, xs.at[0], rows, t, lane)
            return carry

        lax.fori_loop(0, BLK // ROWS, step, 0)

    in3.wait()
    first_collide(3)
    pl.semaphore_wait(barrier, 2)
    sends = [send(1, xs.at[0, 1], xr.at[0, 1], nxt)]
    in0.wait()
    first_collide(0)
    sends.append(send(0, xs.at[0, 0], xr.at[0, 0], prv))

    inc.wait()
    ratio = 0.6 / 1.1
    cs[...] = jnp.zeros((2, 16, TILE), F32)
    for c in range(2):
        row = lax.broadcasted_iota(I32, (2, 64), 0)
        w0 = jnp.where(row == 0, 0.0, 0.5)
        w1 = jnp.where(row == 0, 1.0, 0.5)
        hs = []
        for q in range(19):
            both = cfv[c, q, :, :]
            hs.append(w1 * both + w0 * both[0:1, :])
        rho = functools.reduce(lambda a, b: a + b, hs)
        mom = []
        for axis in range(3):
            plus = functools.reduce(
                lambda a, b: a + b, [hs[q] for q in range(19) if VEL[q][axis] == 1]
            )
            minus = functools.reduce(
                lambda a, b: a + b, [hs[q] for q in range(19) if VEL[q][axis] == -1]
            )
            mom.append(plus - minus)
        inv = 1.0 / rho
        vel = [m * inv for m in mom]
        sq = 1.0 - 1.5 * (vel[0] * vel[0] + vel[1] * vel[1] + vel[2] * vel[2])
        for s, q in enumerate(CROSS[2]):
            proj = None
            for axis in range(3):
                if VEL[q][axis]:
                    term = vel[axis] if VEL[q][axis] == 1 else -vel[axis]
                    proj = term if proj is None else proj + term
            weight = 1.0 / 18.0 if q < 7 else 1.0 / 36.0
            eq = (weight * rho) * (sq + 3.0 * proj + 4.5 * proj * proj)
            val = eq + ratio * (hs[q] - eq)
            for k in range(2):
                cs[k, pl.ds(8 * c + s, 1), 0:64] = val[k : k + 1, :]
    sends.append(send(4, cs, cr, prv))

    in12.wait()
    first_collide(1)
    first_collide(2)

    inn.wait()
    ini.wait()
    eye = lax.broadcasted_iota(I32, (BLK, BLK), 0) == lax.broadcasted_iota(I32, (BLK, BLK), 1)

    def column(row):
        wide = jnp.broadcast_to(row.astype(F32), (BLK, BLK))
        return jnp.sum(jnp.where(eye, wide, 0.0), axis=1, keepdims=True)

    face = [column(nv[d : d + 1, :]) for d in range(6)]
    cb = column(iv[0:1, :])
    quad = column(iv[1:2, :])
    first = (me * BLK).astype(F32)
    slot = (lax.broadcasted_iota(I32, (BLK, 2 * BLK), 1) & (BLK - 1)).astype(F32)
    local = [jnp.where(v >= 0.0, v - first, -1.0) for v in face]
    one = [jnp.where(v == slot, 1.0, 0.0).astype(BF16) for v in local]
    for d in range(2):
        pxl[d] = one[d]
    for d in range(4):
        pyz[d] = one[d + 2]
    for d, shift in ((0, -float(BLK)), (1, float(BLK))):
        far = jnp.where(face[d] >= 0.0, face[d] - first + shift, -1.0)
        pxr[d] = jnp.where(far == slot, 1.0, 0.0).astype(BF16)
    key = jnp.where(cb >= 0.0, 2.0 * quad + cb - 2.0 * (me + 1).astype(F32), -1.0)
    group = ((lax.broadcasted_iota(I32, (BLK, TILE), 1) & 63) >> 3).astype(F32)
    pc[...] = jnp.where(key == group, 1.0, 0.0).astype(BF16)
    for d in range(6):
        there = face[d] >= 0.0
        if d == 2:
            there = there | (cb >= 0.0)
        bits = sum(1 << BIT[q] for q in CROSS[d])
        pw[d] = jnp.broadcast_to(jnp.where(there, -1, ~bits), (BLK, TILE))

    ins.wait()
    static = []
    for t in range(4):
        word = jnp.full((ROWS, TILE), -1, I32)
        for q in range(7, 19):
            axes = [a for a in range(3) if VEL[q][a]]
            masks = [face_lanes(2 * a + (0 if VEL[q][a] < 0 else 1), t, lane) for a in axes]
            if all(m is not None for m in masks):
                word = jnp.where(masks[0] & masks[1], word & ~(1 << BIT[q]), word)
        static.append(word)

    def code_step(r, carry):
        rows = rows_of(r)
        yz = []
        for t in range(4):
            fl = 1 - sv[rows, cols(t)]
            wz = roll(fl, -1) | (fl << 1) | (roll(fl, 1) << 2)
            yz.append(roll(wz, -8) | (wz << 3) | (roll(wz, 8) << 6))
        ones = jnp.full((ROWS, TILE), -1, I32)
        for t in range(4):
            below = yz[t - 1] if t > 0 else ones
            above = yz[t + 1] if t < 3 else ones
            up = roll(jnp.where(lane >= 64, below, yz[t]), 64) << 18
            down = roll(jnp.where(lane < 64, above, yz[t]), 64) & 511
            word = (up | (yz[t] << 9) | down) & static[t]
            for d in range(6):
                m = face_lanes(d, t, lane)
                if m is not None:
                    word = word & jnp.where(m, pw[d, rows, :], -1)
            code[rows, cols(t)] = word
        return carry

    lax.fori_loop(0, BLK // ROWS, code_step, 0)

    sends[2].wait_recv()
    kk = (lane & 7) >> 1
    at = (lane >> 3) & 7
    srow = lax.broadcasted_iota(I32, (ROWS, TILE), 0)
    for k in range(2):
        parts = []
        for quadrant in range(4):
            for c in range(2):
                vals = cr[k, 8 * c : 8 * c + 8, :]
                spread = []
                for t in range(4):
                    idx = kk + (32 * (quadrant // 2) + 4 * (quadrant % 2) + 8 * t)
                    got = jnp.take_along_axis(vals, idx, axis=1, mode="promise_in_bounds")
                    spread.append(jnp.where(at == srow, got, 0.0))
                parts.append(jnp.concatenate(spread, axis=1))
        table = jnp.concatenate(parts, axis=0)
        gc[k] = jnp.dot(pc[...], split(table), preferred_element_type=F32)

    def gather_local(sub):
        for d in range(4):
            g = jnp.dot(pyz[d], split(packs[d]), preferred_element_type=F32)
            if d == 0:
                g = g + gc[sub]
            gh[d] = g
        for d in range(2):
            gxl[d] = jnp.dot(pxl[d], split(xs[sub, d]), preferred_element_type=F32)

    def gather_remote(sub, pair):
        for d in (1, 0):
            pair[d].wait_recv()
            far = jnp.dot(pxr[d], split(xr[sub, d]), preferred_element_type=F32)
            gx[d] = gxl[d] + far

    def second_collide(t):
        def step(r, carry):
            rows = rows_of(r)
            cur = stream(pa, gh, gx, code, rows, t, lane)
            store_post(relax_delta(cur), pb, packs, xs.at[1], rows, t, lane)
            return carry

        lax.fori_loop(0, BLK // ROWS, step, 0)

    def finish(t):
        def step(r, carry):
            rows = rows_of(r)
            cur = stream(pb, gh, gx, code, rows, t, lane)
            wet = (code[rows, cols(t)] & (1 << BIT[0])) != 0
            for q in range(19):
                ov[q, rows, cols(t)] = jnp.where(wet, cur[q], f[q, rows, cols(t)])
            return carry

        lax.fori_loop(0, BLK // ROWS, step, 0)

    gather_local(0)
    second_collide(1)
    second_collide(2)
    gather_remote(0, (sends[1], sends[0]))
    second_collide(3)
    sends.append(send(3, xs.at[1, 1], xr.at[1, 1], nxt))
    second_collide(0)
    sends.append(send(2, xs.at[1, 0], xr.at[1, 0], prv))

    gather_local(1)
    outs = []

    def emit(k, t, w):
        c = pltpu.make_async_copy(tile_of(ov, t, w), tile_of(out, t, w), out_sem.at[k])
        c.start()
        outs.append(c)

    finish(1)
    finish(2)
    emit(0, 1, 2)
    gather_remote(1, (sends[4], sends[3]))
    finish(3)
    emit(1, 3, 1)
    finish(0)
    emit(2, 0, 1)
    for c in sends:
        c.wait_send()
    for c in outs:
        c.wait()


def body(populations, coarse_faces, neighbors, interface, solid):
    n = lax.axis_size("blk")
    pops = jnp.transpose(populations, (1, 0, 2))
    coarse = jnp.transpose(coarse_faces, (0, 2, 1, 3))
    anywhere = pl.BlockSpec(memory_space=pl.ANY)
    vm = pltpu.VMEM
    big = vm((19, BLK, 512), F32)
    done = pl.pallas_call(
        functools.partial(kernel, n),
        out_shape=jax.ShapeDtypeStruct((19, BLK, 512), F32),
        in_specs=[anywhere] * 5,
        out_specs=anywhere,
        scratch_shapes=[
            big,
            big,
            big,
            big,
            vm((4, BLK, 512), F32),
            vm((4, BLK, 512), F32),
            vm((2, BLK, 384), F32),
            vm((2, BLK, 384), F32),
            vm((2, 2, BLK, 384), F32),
            vm((2, 2, BLK, 384), F32),
            vm((2, 19, 2, 64), F32),
            vm((6, BLK), I32),
            vm((2, BLK), I32),
            vm((BLK, 512), I32),
            vm((2, 16, TILE), F32),
            vm((2, 16, TILE), F32),
            vm((2, BLK, 512), F32),
            vm((BLK, 512), I32),
            vm((6, BLK, TILE), I32),
            vm((4, BLK, 2 * BLK), BF16),
            vm((2, BLK, 2 * BLK), BF16),
            vm((2, BLK, 2 * BLK), BF16),
            vm((BLK, TILE), BF16),
            pltpu.SemaphoreType.DMA((7,)),
            pltpu.SemaphoreType.DMA((3,)),
            pltpu.SemaphoreType.DMA((5,)),
            pltpu.SemaphoreType.DMA((5,)),
        ],
        compiler_params=pltpu.CompilerParams(
            collective_id=0, has_side_effects=True, vmem_limit_bytes=40 * 2**20
        ),
    )(pops, coarse, neighbors.T, interface.T, solid)
    return jnp.transpose(done, (1, 0, 2))


def solution(mesh):
    placed = (
        P("blk", None, None),
        P("blk", None, None, None),
        P("blk", None),
        P("blk", None),
        P("blk", None),
    )
    return jax.shard_map(
        body, mesh=mesh, in_specs=placed, out_specs=P("blk", None, None), check_vma=False
    )
```

time: 533 us -> 31.1 us (0.06)
  the two profiles are of different devices: /device:TPU:255 before, /device:TPU:0 now
where the time goes in v1:
time: 31.1 us; the launch traced here: 30.8 us
  Pallas kernels  25.5 us (82%)
  local copies, waits for them, and re-layouts  5.31 us (17%)
    pallas_call x1, Pallas kernels, body(): pl.pallas_call(functools.partial(kernel, n), out_shape=jax.ShapeDtypeStru...  25.5 us
    unnamed x11, local copies, waits for them, and re-layouts  5.31 us

profile of v1, /device:TPU:0, one launch (start us, length us, event | category | flops | bytes accessed | tf_op | source)
XLA Modules:
  0.0 30.8 jit_solution(4429902465783047830)
XLA Ops:
  0.0 0.0 copy-start
  0.0 1.3 %copy-done = f32[32,19,512]{2,0,1:T(8,128)S(1)} copy-done((f32[32,19,512]{2,0,1:T(8,128)S(1)}, f32[32,19,512]{2,0,1:T(8,128)}, u32[]{:S(2)}) %copy-start) | copy-done | bytes 1245208
  1.3 0.0 copy-start.1
  1.3 0.8 %copy-done.1 = s32[32,512]{1,0:T(8,128)S(1)} copy-done((s32[32,512]{1,0:T(8,128)S(1)}, s32[32,512]{1,0:T(8,128)}, u32[]{:S(2)}) %copy-start.1) | copy-done | bytes 65560
  2.1 0.0 copy-start.2
  2.1 0.8 %copy-done.2 = f32[2,2,19,64]{3,1,2,0:T(2,128)S(1)} copy-done((f32[2,2,19,64]{3,1,2,0:T(2,128)S(1)}, f32[2,2,19,64]{3,1,2,0:T(2,128)}, u32[]{:S(2)}) %copy-start.2) | copy-done | bytes 19480
  2.9 0.0 copy-start.3
  2.9 0.7 %copy-done.3 = s32[32,6]{0,1:T(8,128)S(1)} copy-done((s32[32,6]{0,1:T(8,128)S(1)}, s32[32,6]{0,1:T(8,128)}, u32[]{:S(2)}) %copy-start.3) | copy-done | bytes 792
  3.6 0.0 copy-start.4
  3.6 0.7 %copy-done.4 = s32[32,2]{0,1:T(2,128)S(1)} copy-done((s32[32,2]{0,1:T(2,128)S(1)}, s32[32,2]{0,1:T(2,128)}, u32[]{:S(2)}) %copy-start.4) | copy-done | bytes 280
  4.3 25.5 %shard_map.55 = f32[19,32,512]{2,1,0:T(8,128)S(1)} custom-call(f32[19,32,512]{2,1,0:T(8,128)S(1)} %bitcast.6, f32[2,19,2,64]{3,2,1,0:T(2,128)S(1)} %bitcast.7, s32[6,32]{1,0:T(8,128)S(1)} %bitcast.8, s32[2,32]{1,0:T(2,128)S(1)} %bitcast.9, s32[32,512]{1,0:T(8,128)S(1)} %copy-done.1), custom_call_target="tpu_custom_call" | custom-call | tf_op jit(solution)/shard_map/pallas_call | solution.py:530
  29.7 1.0 %copy.7 = f32[32,19,512]{2,0,1:T(8,128)} copy(f32[32,19,512]{2,0,1:T(8,128)S(1)} %bitcast.5) | data formatting | bytes 2490368
Async XLA Ops:
  0.0 1.3 %copy-start = (f32[32,19,512]{2,0,1:T(8,128)S(1)}, f32[32,19,512]{2,0,1:T(8,128)}, u32[]{:S(2)}) copy-start(f32[32,19,512]{2,0,1:T(8,128)} %param.5) | copy-start | bytes 3735556
  1.3 0.8 %copy-start.1 = (s32[32,512]{1,0:T(8,128)S(1)}, s32[32,512]{1,0:T(8,128)}, u32[]{:S(2)}) copy-start(s32[32,512]{1,0:T(8,128)} %solid.1) | copy-start | bytes 196612
  2.1 0.8 %copy-start.2 = (f32[2,2,19,64]{3,1,2,0:T(2,128)S(1)}, f32[2,2,19,64]{3,1,2,0:T(2,128)}, u32[]{:S(2)}) copy-start(f32[2,2,19,64]{3,1,2,0:T(2,128)} %param.6) | copy-start | bytes 58372
  2.9 0.7 %copy-start.3 = (s32[32,6]{0,1:T(8,128)S(1)}, s32[32,6]{0,1:T(8,128)}, u32[]{:S(2)}) copy-start(s32[32,6]{0,1:T(8,128)} %param.7) | copy-start | bytes 2308
  3.6 0.7 %copy-start.4 = (s32[32,2]{0,1:T(2,128)S(1)}, s32[32,2]{0,1:T(2,128)}, u32[]{:S(2)}) copy-start(s32[32,2]{0,1:T(2,128)} %param.8) | copy-start | bytes 772

commit v2 on v1

v2 whole, which is shorter than its diff:
```python
import functools

import jax
import jax.numpy as jnp
import numpy as np
from jax import lax
from jax.experimental import pallas as pl
from jax.experimental.pallas import tpu as pltpu
from jax.sharding import PartitionSpec as P

MESH = pl.DeviceIdType.MESH
F32 = jnp.float32
BF16 = jnp.bfloat16
I32 = jnp.int32

VEL = [
    (0, 0, 0),
    (1, 0, 0),
    (-1, 0, 0),
    (0, 1, 0),
    (0, -1, 0),
    (0, 0, 1),
    (0, 0, -1),
    (1, 1, 0),
    (-1, -1, 0),
    (1, -1, 0),
    (-1, 1, 0),
    (1, 0, 1),
    (-1, 0, -1),
    (1, 0, -1),
    (-1, 0, 1),
    (0, 1, 1),
    (0, -1, -1),
    (0, 1, -1),
    (0, -1, 1),
]
OPP = [VEL.index((-x, -y, -z)) for x, y, z in VEL]
CROSS = [
    [q for q in range(19) if VEL[q][d // 2] == (-1 if d % 2 == 0 else 1)] for d in range(6)
]
BIT = [9 * (x + 1) + 3 * (y + 1) + (z + 1) for x, y, z in VEL]
BLK = 32
TILE = 128


def relax_delta(f):
    s = 1.0 / 0.6
    sx, dx = f[1] + f[2], f[1] - f[2]
    sy, dy = f[3] + f[4], f[3] - f[4]
    sz, dz = f[5] + f[6], f[5] - f[6]
    s7, d7 = f[7] + f[8], f[7] - f[8]
    s9, d9 = f[9] + f[10], f[9] - f[10]
    s11, d11 = f[11] + f[12], f[11] - f[12]
    s13, d13 = f[13] + f[14], f[13] - f[14]
    s15, d15 = f[15] + f[16], f[15] - f[16]
    s17, d17 = f[17] + f[18], f[17] - f[18]
    sa, ta = s7 + s9, s7 - s9
    sb, tb = s11 + s13, s11 - s13
    sc, tc = s15 + s17, s15 - s17
    ax, ay = d7 + d9, d7 - d9
    bx, bz = d11 + d13, d11 - d13
    cy, cz = d15 + d17, d15 - d17
    x2, mx = ax + bx, ax - bx
    y2, my = ay + cy, cy - ay
    z2, mz = bz + cz, bz - cz
    jx, jy, jz = dx + x2, dy + y2, dz + z2
    ab = sa + sb
    s2 = ab + sc
    yz = sy + sz
    s1 = sx + yz
    rho = f[0] + (s1 + s2)
    inv = 1.0 / rho
    ux, uy, uz = jx * inv, jy * inv, jz * inv
    xx, yy, zz = jx * ux, jy * uy, jz * uz
    jj = (xx + yy) + zz
    m1 = (s2 - f[0]) - jj
    m2 = 9.0 * f[0] - 7.0 * s1 - 2.0 * s2 + 5.5 * jj
    c1 = m1 * (19.0 * 1.19 / 2394.0)
    c2 = m2 * (1.4 / 252.0)
    a9 = (sx + sx) - yz
    b9 = ab - (sc + sc)
    e9 = (xx + xx) - (yy + zz)
    c9 = (a9 + b9 - e9) * (s / 36.0)
    c10 = (b9 - 2.0 * a9 + 0.5 * e9) * (1.4 / 72.0)
    a11 = sy - sz
    b11 = sa - sb
    e11 = yy - zz
    c11 = (a11 + b11 - e11) * (s / 12.0)
    c12 = (b11 - 2.0 * a11 + 0.5 * e11) * (1.4 / 24.0)
    c13 = (ta - jx * uy) * (s / 4.0)
    c14 = (tc - jy * uz) * (s / 4.0)
    c15 = (tb - jx * uz) * (s / 4.0)
    g = (5.0 / 3.0) * 1.2 / 40.0
    c4 = (x2 - 2.0 * dx) * g
    c6 = (y2 - 2.0 * dy) * g
    c8 = (z2 - 2.0 * dz) * g
    h = 1.98 / 8.0
    c16, c17, c18 = mx * h, my * h, mz * h
    r0 = 12.0 * c2 - 30.0 * c1
    ra = -11.0 * c1 - 4.0 * c2
    rd = 8.0 * c1 + c2
    p9 = c9 - 2.0 * c10
    p11 = c11 - 2.0 * c12
    n9 = c9 + c10
    n11 = c11 + c12
    ex = ra + 2.0 * p9
    et = ra - p9
    ey, ez = et + p11, et - p11
    rt = rd + n9
    exy, exz = rt + n11, rt - n11
    eyz = rd - 2.0 * n9
    ox, oy, oz = -4.0 * c4, -4.0 * c6, -4.0 * c8
    xa, ya = c4 + c16, c6 - c17
    xb, zb = c4 - c16, c8 + c18
    yc, zc = c6 + c17, c8 - c18
    e7, e9_ = exy + c13, exy - c13
    e11_, e13 = exz + c15, exz - c15
    e15, e17 = eyz + c14, eyz - c14
    o7, o9 = xa + ya, xa - ya
    o11, o13 = xb + zb, xb - zb
    o15, o17 = yc + zc, yc - zc
    out = [f[0] - r0]
    for q, even, odd in (
        (1, ex, ox),
        (3, ey, oy),
        (5, ez, oz),
        (7, e7, o7),
        (9, e9_, o9),
        (11, e11_, o11),
        (13, e13, o13),
        (15, e15, o15),
        (17, e17, o17),
    ):
        out.append(f[q] - (even + odd))
        out.append(f[q + 1] - (even - odd))
    return out


def split(x):
    hi = x.astype(BF16)
    lo = (x - hi.astype(F32)).astype(BF16)
    return jnp.concatenate([hi, lo], axis=0)


def roll(x, by):
    by %= TILE
    return pltpu.roll(x, by, 1) if by else x


def lanes():
    return lax.broadcasted_iota(I32, (BLK, TILE), 1)


def face_lanes(d, t, lane):
    if d == 0:
        return lane >= 64 if t == 3 else None
    if d == 1:
        return lane < 64 if t == 0 else None
    pos = ((lane >> 3) & 7) if d < 4 else (lane & 7)
    return pos == (7 if d % 2 == 0 else 0)


def cols(t):
    return pl.ds(t * TILE, TILE)


def store_post(post, ref, packs, xs, t, lane):
    for q in range(19):
        ref[q, :, cols(t)] = post[q]
    high = lane & 7
    mid = (lane >> 3) & 7
    for d in range(2, 6):
        acc = post[CROSS[d][0]]
        for s in range(1, 5):
            step = (8 if d < 4 else 1) * s
            pos = mid if d < 4 else high
            by, at = (step, s) if d % 2 == 0 else (-step, 7 - s)
            acc = jnp.where(pos == at, roll(post[CROSS[d][s]], by), acc)
        packs[d - 2, :, cols(t)] = acc
    if t in (0, 3):
        d = 0 if t == 0 else 1
        keep = lane < 64 if t == 0 else lane >= 64
        for s in range(2):
            a, b = CROSS[d][2 * s], CROSS[d][2 * s + 1]
            xs[d, :, cols(s)] = jnp.where(keep, post[a], roll(post[b], 64))
        xs[d, :, cols(2)] = post[CROSS[d][4]]


def stream(ref, gh, gx, code_ref, t, lane):
    post = [ref[q, :, cols(t)] for q in range(19)]
    code = code_ref[:, cols(t)]
    upper = lane >= 64

    def merged(ex, here, load, edge):
        if ex == 0:
            return here
        near = t - ex
        if 0 <= near <= 3:
            other = load(near)
        else:
            other = edge
        if other is None:
            return here
        return jnp.where(upper, other, here) if ex == 1 else jnp.where(upper, here, other)

    out = [post[0]]
    for q in range(1, 19):
        ex, ey, ez = VEL[q]
        edge = None
        if ex != 0 and not 0 <= t - ex <= 3:
            d = 0 if ex == -1 else 1
            n = CROSS[d].index(q)
            edge = gx[d, :, cols(n // 2)]
            if n % 2:
                edge = roll(edge, 64)
        base = 64 * ex
        src = merged(ex, post[q], lambda u: ref[q, :, cols(u)], edge)
        moved = roll(src, base + 8 * ey + ez)
        for d, comp in ((2 if ey < 0 else 3, ey), (4 if ez < 0 else 5, ez)):
            if comp == 0:
                continue
            s = CROSS[d].index(q)
            if d < 4:
                off = (56 - 8 * s) * (1 if d == 2 else -1) + base + ez
            else:
                off = (7 - s) * (1 if d == 4 else -1) + base + 8 * ey
            g = merged(
                ex, gh[d - 2, :, cols(t)], lambda u: gh[d - 2, :, cols(u)], None
            )
            moved = jnp.where(face_lanes(d, t, lane), roll(g, off), moved)
        usable = (code & (1 << BIT[q])) != 0
        out.append(jnp.where(usable, moved, post[OPP[q]]))
    return out


def coarse_ghost(cfv, cs):
    ratio = 0.6 / 1.1
    cs[...] = jnp.zeros((2, 16, TILE), F32)
    row = lax.broadcasted_iota(I32, (2, 64), 0)
    w0 = jnp.where(row == 0, 0.0, 0.5)
    w1 = jnp.where(row == 0, 1.0, 0.5)

    def total(items):
        return functools.reduce(lambda a, b: a + b, items)

    for c in range(2):
        hs = []
        for q in range(19):
            both = cfv[c, q, :, :]
            hs.append(w1 * both + w0 * both[0:1, :])
        rho = total(hs)
        inv = 1.0 / rho
        vel = []
        for axis in range(3):
            plus = total([hs[q] for q in range(19) if VEL[q][axis] == 1])
            minus = total([hs[q] for q in range(19) if VEL[q][axis] == -1])
            vel.append((plus - minus) * inv)
        sq = 1.0 - 1.5 * (vel[0] * vel[0] + vel[1] * vel[1] + vel[2] * vel[2])
        for s, q in enumerate(CROSS[2]):
            proj = total(
                [v if e == 1 else -v for v, e in zip(vel, VEL[q]) if e]
            )
            weight = 1.0 / 18.0 if q < 7 else 1.0 / 36.0
            eq = (weight * rho) * (sq + 3.0 * proj + 4.5 * proj * proj)
            val = eq + ratio * (hs[q] - eq)
            for k in range(2):
                cs[k, pl.ds(8 * c + s, 1), 0:64] = val[k : k + 1, :]


def build_tables(me, nv, iv, pyz, pxl, pxr, pc, pw):
    row, col = (lax.broadcasted_iota(I32, (BLK, BLK), a) for a in (0, 1))
    eye = row == col

    def column(vals):
        wide = jnp.broadcast_to(vals.astype(F32), (BLK, BLK))
        return jnp.sum(jnp.where(eye, wide, 0.0), axis=1, keepdims=True)

    face = [column(nv[d : d + 1, :]) for d in range(6)]
    cb = column(iv[0:1, :])
    quad = column(iv[1:2, :])
    first = (me * BLK).astype(F32)
    slot = (lax.broadcasted_iota(I32, (BLK, 2 * BLK), 1) & (BLK - 1)).astype(F32)
    for d in range(6):
        local = jnp.where(face[d] >= 0.0, face[d] - first, -1.0)
        one = jnp.where(local == slot, 1.0, 0.0).astype(BF16)
        if d < 2:
            pxl[d] = one
            shift = -float(BLK) if d == 0 else float(BLK)
            there = jnp.where(face[d] >= 0.0, face[d] - first + shift, -1.0)
            pxr[d] = jnp.where(there == slot, 1.0, 0.0).astype(BF16)
        else:
            pyz[d - 2] = one
    key = jnp.where(cb >= 0.0, 2.0 * quad + cb - 2.0 * (me + 1).astype(F32), -1.0)
    group = ((lax.broadcasted_iota(I32, (BLK, TILE), 1) & 63) >> 3).astype(F32)
    pc[...] = jnp.where(key == group, 1.0, 0.0).astype(BF16)
    for d in range(6):
        there = face[d] >= 0.0
        if d == 2:
            there = there | (cb >= 0.0)
        bits = sum(1 << BIT[q] for q in CROSS[d])
        pw[d] = jnp.broadcast_to(jnp.where(there, -1, ~bits), (BLK, TILE))


def build_code(sv, pw, code, lane):
    yz = []
    for t in range(4):
        fl = 1 - sv[:, cols(t)]
        wz = roll(fl, -1) | (fl << 1) | (roll(fl, 1) << 2)
        yz.append(roll(wz, -8) | (wz << 3) | (roll(wz, 8) << 6))
    ones = jnp.full((BLK, TILE), -1, I32)
    row = lax.broadcasted_iota(I32, (8, TILE), 1)
    for t in range(4):
        static = jnp.full((8, TILE), -1, I32)
        for q in range(7, 19):
            axes = [a for a in range(3) if VEL[q][a]]
            masks = [face_lanes(2 * a + (0 if VEL[q][a] < 0 else 1), t, row) for a in axes]
            if all(m is not None for m in masks):
                static = jnp.where(masks[0] & masks[1], static & ~(1 << BIT[q]), static)
        static = jnp.concatenate([static] * (BLK // 8), axis=0)
        below = yz[t - 1] if t > 0 else ones
        above = yz[t + 1] if t < 3 else ones
        up = roll(jnp.where(lane >= 64, below, yz[t]), 64) << 18
        down = roll(jnp.where(lane < 64, above, yz[t]), 64) & 511
        word = (up | (yz[t] << 9) | down) & static
        for d in range(6):
            m = face_lanes(d, t, lane)
            if m is not None:
                word = word & jnp.where(m, pw[d], -1)
        code[:, cols(t)] = word


def spread_coarse(cr, pc, gc):
    lane = lax.broadcasted_iota(I32, (8, TILE), 1)
    srow = lax.broadcasted_iota(I32, (8, TILE), 0)
    half = (lane & 7) >> 1
    at = (lane >> 3) & 7
    for k in range(2):
        parts = []
        for quadrant in range(4):
            for c in range(2):
                vals = cr[k, 8 * c : 8 * c + 8, :]
                wide = []
                for t in range(4):
                    idx = half + (32 * (quadrant // 2) + 4 * (quadrant % 2) + 8 * t)
                    got = jnp.take_along_axis(vals, idx, axis=1, mode="promise_in_bounds")
                    wide.append(jnp.where(at == srow, got, 0.0))
                parts.append(jnp.concatenate(wide, axis=1))
        table = jnp.concatenate(parts, axis=0)
        gc[k] = jnp.dot(pc[...], split(table), preferred_element_type=F32)


def kernel(
    n,
    pops,
    coarse,
    nbr,
    itf,
    solid,
    out,
    f,
    pa,
    pb,
    packs,
    gh,
    gxl,
    gx,
    xs,
    xr,
    cfv,
    nv,
    iv,
    sv,
    cs,
    cr,
    gc,
    code,
    pw,
    pyz,
    pxl,
    pxr,
    pc,
    in_sem,
    send_sem,
    recv_sem,
):
    me = lax.axis_index("blk")
    nxt = lax.rem(me + 1, n)
    prv = lax.rem(me + n - 1, n)
    lane = lanes()

    def remote(k, src, dst, peer):
        return pltpu.make_async_remote_copy(
            src_ref=src,
            dst_ref=dst,
            send_sem=send_sem.at[k],
            recv_sem=recv_sem.at[k],
            device_id=(peer,),
            device_id_type=MESH,
        )

    def x_copy(sub, k):
        return remote(2 * sub + k, xs.at[sub, k], xr.at[sub, k], nxt if k else prv)

    def c_copy():
        return remote(4, cs, cr, prv)

    def run(even):
        near, far = (0, 1) if even else (1, 0)
        near_tile, far_tile = (3, 0) if even else (0, 3)
        peers = {0: nxt, 1: prv}
        has_far = me > 0 if even else me < n - 1

        barrier = pltpu.get_barrier_semaphore()

        def greet(peer):
            pl.semaphore_signal(barrier, inc=1, device_id=(peer,), device_id_type=MESH)

        greet(peers[near])
        pl.when(has_far)(lambda: greet(peers[far]))

        def fetch(k, src, dst):
            c = pltpu.make_async_copy(src, dst, in_sem.at[k])
            c.start()
            return c

        def fetch_tiles(k, t, w=1):
            part = pl.ds(t * TILE, w * TILE)
            return fetch(k, pops.at[:, :, part], f.at[:, :, part])

        in_c = fetch(0, coarse, cfv)
        in_far = fetch_tiles(1, far_tile)
        in_near = fetch_tiles(2, near_tile)
        in_n = fetch(3, nbr, nv)
        in_i = fetch(4, itf, iv)
        in_mid = fetch_tiles(5, 1, 2)
        in_s = fetch(6, solid, sv)

        def first_collide(t):
            post = relax_delta([f[q, :, cols(t)] for q in range(19)])
            store_post(post, pa, packs, xs.at[0], t, lane)

        def second_collide(t):
            cur = stream(pa, gh, gx, code, t, lane)
            store_post(relax_delta(cur), pb, packs, xs.at[1], t, lane)

        def finish(t):
            cur = stream(pb, gh, gx, code, t, lane)
            wet = (code[:, cols(t)] & (1 << BIT[0])) != 0
            for q in range(19):
                out[q, :, cols(t)] = jnp.where(wet, cur[q], f[q, :, cols(t)])

        def gather_local(sub):
            for d in range(4):
                g = jnp.dot(pyz[d], split(packs[d]), preferred_element_type=F32)
                gh[d] = g + gc[sub] if d == 0 else g
            for d in range(2):
                gxl[d] = jnp.dot(pxl[d], split(xs[sub, d]), preferred_element_type=F32)

        def take(sub, d):
            x_copy(sub, d).wait_recv()
            got = jnp.dot(pxr[d], split(xr[sub, d]), preferred_element_type=F32)
            gx[d] = gxl[d] + got

        def take_far(sub):
            pl.when(has_far)(lambda: take(sub, far))

            @pl.when(jnp.logical_not(has_far))
            def _():
                gx[far] = gxl[far]

        def send_near(sub):
            x_copy(sub, 1 - near).start()

        def send_far(sub):
            pl.when(has_far)(lambda: x_copy(sub, 1 - far).start())

        in_c.wait()
        coarse_ghost(cfv, cs)
        in_far.wait()
        first_collide(far_tile)
        pl.semaphore_wait(barrier, 1 + has_far.astype(I32))
        if even:
            pl.when(has_far)(lambda: c_copy().start())
        else:
            c_copy().start()
        send_far(0)
        in_near.wait()
        first_collide(near_tile)
        send_near(0)

        in_n.wait()
        in_i.wait()
        build_tables(me, nv, iv, pyz, pxl, pxr, pc, pw)
        in_mid.wait()
        first_collide(1)
        first_collide(2)
        in_s.wait()
        build_code(sv, pw, code, lane)

        if even:
            c_copy().wait_recv()
        else:
            pl.when(has_far)(lambda: c_copy().wait_recv())

            @pl.when(jnp.logical_not(has_far))
            def _():
                cr[...] = jnp.zeros((2, 16, TILE), F32)

        spread_coarse(cr, pc, gc)
        gather_local(0)
        if not even:
            second_collide(1)
            second_collide(2)
        take(0, near)
        second_collide(near_tile)
        send_near(1)
        if even:
            second_collide(1)
            second_collide(2)
        take_far(0)
        second_collide(far_tile)
        send_far(1)

        gather_local(1)
        finish(1)
        finish(2)
        take(1, near)
        finish(near_tile)
        take_far(1)
        finish(far_tile)

        for sub in range(2):
            x_copy(sub, 1 - near).wait_send()
        if not even:
            c_copy().wait_send()

        @pl.when(has_far)
        def _():
            for sub in range(2):
                x_copy(sub, 1 - far).wait_send()
            if even:
                c_copy().wait_send()

    is_even = lax.rem(me, 2) == 0
    pl.when(is_even)(lambda: run(True))
    pl.when(jnp.logical_not(is_even))(lambda: run(False))


def body(populations, coarse_faces, neighbors, interface, solid):
    n = lax.axis_size("blk")
    pops = jnp.transpose(populations, (1, 0, 2))
    coarse = jnp.transpose(coarse_faces, (0, 2, 1, 3))
    ins = (pops, coarse, neighbors.T, interface.T, solid)
    ins = [pltpu.with_memory_space_constraint(v, pltpu.HBM) for v in ins]
    anywhere = pl.BlockSpec(memory_space=pl.ANY)
    vm = pltpu.VMEM
    big = vm((19, BLK, 512), F32)
    done = pl.pallas_call(
        functools.partial(kernel, n),
        out_shape=jax.ShapeDtypeStruct((19, BLK, 512), F32),
        in_specs=[anywhere] * 5,
        out_specs=pl.BlockSpec(memory_space=pltpu.VMEM),
        scratch_shapes=[
            big,
            big,
            big,
            vm((4, BLK, 512), F32),
            vm((4, BLK, 512), F32),
            vm((2, BLK, 384), F32),
            vm((2, BLK, 384), F32),
            vm((2, 2, BLK, 384), F32),
            vm((2, 2, BLK, 384), F32),
            vm((2, 19, 2, 64), F32),
            vm((6, BLK), I32),
            vm((2, BLK), I32),
            vm((BLK, 512), I32),
            vm((2, 16, TILE), F32),
            vm((2, 16, TILE), F32),
            vm((2, BLK, 512), F32),
            vm((BLK, 512), I32),
            vm((6, BLK, TILE), I32),
            vm((4, BLK, 2 * BLK), BF16),
            vm((2, BLK, 2 * BLK), BF16),
            vm((2, BLK, 2 * BLK), BF16),
            vm((BLK, TILE), BF16),
            pltpu.SemaphoreType.DMA((7,)),
            pltpu.SemaphoreType.DMA((5,)),
            pltpu.SemaphoreType.DMA((5,)),
        ],
        compiler_params=pltpu.CompilerParams(
            collective_id=0, has_side_effects=True, vmem_limit_bytes=40 * 2**20
        ),
    )(*ins)
    return jnp.transpose(done, (1, 0, 2))


def solution(mesh):
    placed = (
        P("blk", None, None),
        P("blk", None, None, None),
        P("blk", None),
        P("blk", None),
        P("blk", None),
    )
    return jax.shard_map(
        body, mesh=mesh, in_specs=placed, out_specs=P("blk", None, None), check_vma=False
    )
```

time: 31.1 us -> 19.4 us (0.62)
  the two profiles are of different devices: /device:TPU:0 before, /device:TPU:256 now
where the time goes in v2:
time: 19.4 us; the launch traced here: 19.3 us
  Pallas kernels  18.2 us (94%)
  local copies, waits for them, and re-layouts  1.04 us (5%)
    pallas_call x1, Pallas kernels, body(): pl.pallas_call(functools.partial(kernel, n), out_shape=jax.ShapeDtypeStru...  18.2 us
    unnamed x1, local copies, waits for them, and re-layouts  1.04 us

profile of v2, /device:TPU:256, one launch (start us, length us, event | category | flops | bytes accessed | tf_op | source)
XLA Modules:
  0.0 19.3 jit_solution(8863957014344373519)
XLA Ops:
  0.0 18.2 %shard_map.55 = f32[19,32,512]{2,1,0:T(8,128)S(1)} custom-call(f32[19,32,512]{2,1,0:T(8,128)} %bitcast.6, f32[2,19,2,64]{3,2,1,0:T(2,128)} %bitcast.7, s32[6,32]{1,0:T(8,128)} %bitcast.8, s32[2,32]{1,0:T(2,128)} %bitcast.9, s32[32,512]{1,0:T(8,128)} %solid.1), custom_call_target="tpu_custom_call" | custom-call | tf_op jit(solution)/shard_map/pallas_call | solution.py:558
  18.2 1.0 %copy.7 = f32[32,19,512]{2,0,1:T(8,128)} copy(f32[32,19,512]{2,0,1:T(8,128)S(1)} %bitcast.5) | data formatting | bytes 2490368

commit v3 on v2

--- a/solution.py
+++ b/solution.py
@@ -39,6 +39,7 @@
     [q for q in range(19) if VEL[q][d // 2] == (-1 if d % 2 == 0 else 1)] for d in range(6)
 ]
 BIT = [9 * (x + 1) + 3 * (y + 1) + (z + 1) for x, y, z in VEL]
+OTHERS = [[q for q in range(19) if q not in CROSS[1 - d]] for d in range(2)]
 BLK = 32
 TILE = 128
 
@@ -164,55 +165,70 @@
     return pl.ds(t * TILE, TILE)
 
 
-def store_post(post, ref, packs, xs, t, lane):
+def pack_halves(vals, d, lane):
+    keep = lane < 64 if d == 0 else lane >= 64
+    tiles = []
+    for s in range(0, len(vals), 2):
+        tiles.append(jnp.where(keep, vals[s], roll(vals[s + 1], 64)))
+    return tiles
+
+
+def layer(ref, d, n):
+    tile = ref[d, :, cols(n // 2)]
+    return roll(tile, 64) if n % 2 else tile
+
+
+def store_post(post, ref, packs, xs, key, t, lane):
     for q in range(19):
         ref[q, :, cols(t)] = post[q]
-    high = lane & 7
+    low = lane & 7
     mid = (lane >> 3) & 7
     for d in range(2, 6):
         acc = post[CROSS[d][0]]
         for s in range(1, 5):
             step = (8 if d < 4 else 1) * s
-            pos = mid if d < 4 else high
+            pos = mid if d < 4 else low
             by, at = (step, s) if d % 2 == 0 else (-step, 7 - s)
             acc = jnp.where(pos == at, roll(post[CROSS[d][s]], by), acc)
         packs[d - 2, :, cols(t)] = acc
     if t in (0, 3):
         d = 0 if t == 0 else 1
-        keep = lane < 64 if t == 0 else lane >= 64
-        for s in range(2):
-            a, b = CROSS[d][2 * s], CROSS[d][2 * s + 1]
-            xs[d, :, cols(s)] = jnp.where(keep, post[a], roll(post[b], 64))
-        xs[d, :, cols(2)] = post[CROSS[d][4]]
-
-
-def stream(ref, gh, gx, code_ref, t, lane):
+        vals = [post[q] for q in CROSS[d]] + [key]
+        for s, tile in enumerate(pack_halves(vals, d, lane)):
+            xs[d, :, cols(s)] = tile
+
+
+def y_offset(d, s):
+    return (56 - 8 * s) if d == 2 else (8 * s - 56)
+
+
+def stream(ref, gh, gx, code_ref, t, lane, qs=tuple(range(19)), have=None):
     post = [ref[q, :, cols(t)] for q in range(19)]
     code = code_ref[:, cols(t)]
     upper = lane >= 64
 
     def merged(ex, here, load, edge):
-        if ex == 0:
+        if ex == 0 or gx is None:
             return here
         near = t - ex
-        if 0 <= near <= 3:
-            other = load(near)
-        else:
-            other = edge
+        other = load(near) if 0 <= near <= 3 else edge
         if other is None:
             return here
         return jnp.where(upper, other, here) if ex == 1 else jnp.where(upper, here, other)
 
-    out = [post[0]]
-    for q in range(1, 19):
+    out = []
+    for q in qs:
+        if have and q in have:
+            out.append(have[q])
+            continue
+        if q == 0:
+            out.append(post[0])
+            continue
         ex, ey, ez = VEL[q]
         edge = None
-        if ex != 0 and not 0 <= t - ex <= 3:
+        if gx is not None and ex != 0 and not 0 <= t - ex <= 3:
             d = 0 if ex == -1 else 1
-            n = CROSS[d].index(q)
-            edge = gx[d, :, cols(n // 2)]
-            if n % 2:
-                edge = roll(edge, 64)
+            edge = gx[d, CROSS[d].index(q), :, :]
         base = 64 * ex
         src = merged(ex, post[q], lambda u: ref[q, :, cols(u)], edge)
         moved = roll(src, base + 8 * ey + ez)
@@ -221,16 +237,45 @@
                 continue
             s = CROSS[d].index(q)
             if d < 4:
-                off = (56 - 8 * s) * (1 if d == 2 else -1) + base + ez
+                off = y_offset(d, s) + base + ez
             else:
                 off = (7 - s) * (1 if d == 4 else -1) + base + 8 * ey
-            g = merged(
-                ex, gh[d - 2, :, cols(t)], lambda u: gh[d - 2, :, cols(u)], None
-            )
+            g = merged(ex, gh[d - 2, :, cols(t)], lambda u: gh[d - 2, :, cols(u)], None)
             moved = jnp.where(face_lanes(d, t, lane), roll(g, off), moved)
         usable = (code & (1 << BIT[q])) != 0
         out.append(jnp.where(usable, moved, post[OPP[q]]))
     return out
+
+
+def far_edge(ref, d, g0, g1, ct, lane):
+    t = 3 if d == 0 else 0
+    cur = [None] * 19
+    for n, q in enumerate(OTHERS[d]):
+        cur[q] = layer(g1, d, n)
+    for q in CROSS[1 - d]:
+        ex, ey, ez = VEL[q]
+        moved = roll(ref[q, :, cols(t)], 64 + 8 * ey + ez)
+        back = layer(g0, d, CROSS[d].index(OPP[q]))
+        for f, comp in ((2 if ey < 0 else 3, ey), (4 if ez < 0 else 5, ez)):
+            if comp:
+                moved = jnp.where(face_lanes(f, t, lane), back, moved)
+        cur[q] = moved
+    if d == 1:
+        tile = g0[d, :, cols(2)]
+        key = jnp.where(lane >= 64, roll(tile, 64), tile)
+        group = ((lane & 63) >> 3).astype(F32)
+        pick = jnp.where(key == group, 1.0, 0.0).astype(BF16)
+        ghost = jnp.dot(pick, ct[...], preferred_element_type=F32)
+        for s, q in enumerate(CROSS[2]):
+            ex, ey, ez = VEL[q]
+            if ex < 0:
+                continue
+            at = face_lanes(2, 3, lane) & (key >= 0.0)
+            if ez:
+                at = at & jnp.logical_not(face_lanes(4 if ez < 0 else 5, 3, lane))
+            cur[q] = jnp.where(at, roll(ghost, y_offset(2, s) + 64 * ex + ez), cur[q])
+    post = relax_delta(cur)
+    return [post[q] for q in CROSS[d]]
 
 
 def coarse_ghost(cfv, cs):
@@ -267,7 +312,7 @@
                 cs[k, pl.ds(8 * c + s, 1), 0:64] = val[k : k + 1, :]
 
 
-def build_tables(me, nv, iv, pyz, pxl, pxr, pc, pw):
+def build_tables(me, nv, iv, pyz, pxl, pxr, pc, pw, rm, keys):
     row, col = (lax.broadcasted_iota(I32, (BLK, BLK), a) for a in (0, 1))
     eye = row == col
 
@@ -288,9 +333,12 @@
             shift = -float(BLK) if d == 0 else float(BLK)
             there = jnp.where(face[d] >= 0.0, face[d] - first + shift, -1.0)
             pxr[d] = jnp.where(there == slot, 1.0, 0.0).astype(BF16)
+            mine = (there >= 0.0) & (there < float(BLK))
+            rm[d] = jnp.broadcast_to(jnp.where(mine, 1.0, 0.0), (BLK, TILE))
         else:
             pyz[d - 2] = one
     key = jnp.where(cb >= 0.0, 2.0 * quad + cb - 2.0 * (me + 1).astype(F32), -1.0)
+    keys[...] = jnp.broadcast_to(key, (BLK, TILE))
     group = ((lax.broadcasted_iota(I32, (BLK, TILE), 1) & 63) >> 3).astype(F32)
     pc[...] = jnp.where(key == group, 1.0, 0.0).astype(BF16)
     for d in range(6):
@@ -329,24 +377,22 @@
         code[:, cols(t)] = word
 
 
-def spread_coarse(cr, pc, gc):
+def coarse_table(src, k, tiles):
     lane = lax.broadcasted_iota(I32, (8, TILE), 1)
     srow = lax.broadcasted_iota(I32, (8, TILE), 0)
     half = (lane & 7) >> 1
     at = (lane >> 3) & 7
-    for k in range(2):
-        parts = []
-        for quadrant in range(4):
-            for c in range(2):
-                vals = cr[k, 8 * c : 8 * c + 8, :]
-                wide = []
-                for t in range(4):
-                    idx = half + (32 * (quadrant // 2) + 4 * (quadrant % 2) + 8 * t)
-                    got = jnp.take_along_axis(vals, idx, axis=1, mode="promise_in_bounds")
-                    wide.append(jnp.where(at == srow, got, 0.0))
-                parts.append(jnp.concatenate(wide, axis=1))
-        table = jnp.concatenate(parts, axis=0)
-        gc[k] = jnp.dot(pc[...], split(table), preferred_element_type=F32)
+    parts = []
+    for quadrant in range(4):
+        for c in range(2):
+            vals = src[k, 8 * c : 8 * c + 8, :]
+            wide = []
+            for t in tiles:
+                idx = half + (32 * (quadrant // 2) + 4 * (quadrant % 2) + 8 * t)
+                got = jnp.take_along_axis(vals, idx, axis=1, mode="promise_in_bounds")
+                wide.append(jnp.where(at == srow, got, 0.0))
+            parts.append(jnp.concatenate(wide, axis=1))
+    return split(jnp.concatenate(parts, axis=0))
 
 
 def kernel(
@@ -362,10 +408,14 @@
     pb,
     packs,
     gh,
-    gxl,
+    g0,
+    g1,
     gx,
-    xs,
-    xr,
+    xs0,
+    xr0,
+    xs1,
+    xr1,
+    xl,
     cfv,
     nv,
     iv,
@@ -375,175 +425,206 @@
     gc,
     code,
     pw,
+    rm,
+    keys,
     pyz,
     pxl,
     pxr,
     pc,
+    ct,
     in_sem,
     send_sem,
     recv_sem,
 ):
     me = lax.axis_index("blk")
-    nxt = lax.rem(me + 1, n)
-    prv = lax.rem(me + n - 1, n)
+    peers = (lax.rem(me + n - 1, n), lax.rem(me + 1, n))
+    has = (me > 0, me < n - 1)
     lane = lanes()
-
-    def remote(k, src, dst, peer):
+    barrier = pltpu.get_barrier_semaphore()
+
+    def both(act):
+        for k in range(2):
+            pl.when(has[k])(functools.partial(act, k))
+
+    def greet(k):
+        pl.semaphore_signal(barrier, inc=1, device_id=(peers[k],), device_id_type=MESH)
+
+    both(greet)
+
+    def fetch(k, src, dst):
+        c = pltpu.make_async_copy(src, dst, in_sem.at[k])
+        c.start()
+        return c
+
+    def fetch_tiles(k, t, w=1):
+        part = pl.ds(t * TILE, w * TILE)
+        return fetch(k, pops.at[:, :, part], f.at[:, :, part])
+
+    in_n = fetch(0, nbr, nv)
+    in_i = fetch(1, itf, iv)
+    in_c = fetch(2, coarse, cfv)
+    in_s = fetch(3, solid, sv)
+    in_3 = fetch_tiles(4, 3)
+    in_0 = fetch_tiles(5, 0)
+    in_m = fetch_tiles(6, 1, 2)
+
+    def remote(sem, src, dst, k):
         return pltpu.make_async_remote_copy(
             src_ref=src,
             dst_ref=dst,
-            send_sem=send_sem.at[k],
-            recv_sem=recv_sem.at[k],
-            device_id=(peer,),
+            send_sem=send_sem.at[sem],
+            recv_sem=recv_sem.at[sem],
+            device_id=(peers[k],),
             device_id_type=MESH,
         )
 
-    def x_copy(sub, k):
-        return remote(2 * sub + k, xs.at[sub, k], xr.at[sub, k], nxt if k else prv)
-
-    def c_copy():
-        return remote(4, cs, cr, prv)
-
-    def run(even):
-        near, far = (0, 1) if even else (1, 0)
-        near_tile, far_tile = (3, 0) if even else (0, 3)
-        peers = {0: nxt, 1: prv}
-        has_far = me > 0 if even else me < n - 1
-
-        barrier = pltpu.get_barrier_semaphore()
-
-        def greet(peer):
-            pl.semaphore_signal(barrier, inc=1, device_id=(peer,), device_id_type=MESH)
-
-        greet(peers[near])
-        pl.when(has_far)(lambda: greet(peers[far]))
-
-        def fetch(k, src, dst):
-            c = pltpu.make_async_copy(src, dst, in_sem.at[k])
-            c.start()
-            return c
-
-        def fetch_tiles(k, t, w=1):
-            part = pl.ds(t * TILE, w * TILE)
-            return fetch(k, pops.at[:, :, part], f.at[:, :, part])
-
-        in_c = fetch(0, coarse, cfv)
-        in_far = fetch_tiles(1, far_tile)
-        in_near = fetch_tiles(2, near_tile)
-        in_n = fetch(3, nbr, nv)
-        in_i = fetch(4, itf, iv)
-        in_mid = fetch_tiles(5, 1, 2)
-        in_s = fetch(6, solid, sv)
-
-        def first_collide(t):
-            post = relax_delta([f[q, :, cols(t)] for q in range(19)])
-            store_post(post, pa, packs, xs.at[0], t, lane)
-
-        def second_collide(t):
-            cur = stream(pa, gh, gx, code, t, lane)
-            store_post(relax_delta(cur), pb, packs, xs.at[1], t, lane)
-
-        def finish(t):
-            cur = stream(pb, gh, gx, code, t, lane)
-            wet = (code[:, cols(t)] & (1 << BIT[0])) != 0
-            for q in range(19):
-                out[q, :, cols(t)] = jnp.where(wet, cur[q], f[q, :, cols(t)])
-
-        def gather_local(sub):
-            for d in range(4):
-                g = jnp.dot(pyz[d], split(packs[d]), preferred_element_type=F32)
-                gh[d] = g + gc[sub] if d == 0 else g
-            for d in range(2):
-                gxl[d] = jnp.dot(pxl[d], split(xs[sub, d]), preferred_element_type=F32)
-
-        def take(sub, d):
-            x_copy(sub, d).wait_recv()
-            got = jnp.dot(pxr[d], split(xr[sub, d]), preferred_element_type=F32)
-            gx[d] = gxl[d] + got
-
-        def take_far(sub):
-            pl.when(has_far)(lambda: take(sub, far))
-
-            @pl.when(jnp.logical_not(has_far))
-            def _():
-                gx[far] = gxl[far]
-
-        def send_near(sub):
-            x_copy(sub, 1 - near).start()
-
-        def send_far(sub):
-            pl.when(has_far)(lambda: x_copy(sub, 1 - far).start())
-
-        in_c.wait()
-        coarse_ghost(cfv, cs)
-        in_far.wait()
-        first_collide(far_tile)
-        pl.semaphore_wait(barrier, 1 + has_far.astype(I32))
-        if even:
-            pl.when(has_far)(lambda: c_copy().start())
-        else:
-            c_copy().start()
-        send_far(0)
-        in_near.wait()
-        first_collide(near_tile)
-        send_near(0)
-
-        in_n.wait()
-        in_i.wait()
-        build_tables(me, nv, iv, pyz, pxl, pxr, pc, pw)
-        in_mid.wait()
-        first_collide(1)
-        first_collide(2)
-        in_s.wait()
-        build_code(sv, pw, code, lane)
-
-        if even:
-            c_copy().wait_recv()
-        else:
-            pl.when(has_far)(lambda: c_copy().wait_recv())
-
-            @pl.when(jnp.logical_not(has_far))
-            def _():
-                cr[...] = jnp.zeros((2, 16, TILE), F32)
-
-        spread_coarse(cr, pc, gc)
-        gather_local(0)
-        if not even:
-            second_collide(1)
-            second_collide(2)
-        take(0, near)
-        second_collide(near_tile)
-        send_near(1)
-        if even:
-            second_collide(1)
-            second_collide(2)
-        take_far(0)
-        second_collide(far_tile)
-        send_far(1)
-
-        gather_local(1)
-        finish(1)
-        finish(2)
-        take(1, near)
-        finish(near_tile)
-        take_far(1)
-        finish(far_tile)
-
-        for sub in range(2):
-            x_copy(sub, 1 - near).wait_send()
-        if not even:
-            c_copy().wait_send()
-
-        @pl.when(has_far)
+    def copy_a(k):
+        return remote(k, xs0.at[k], xr0.at[k], k)
+
+    def copy_b(k):
+        return remote(2 + k, xs1.at[k], xr1.at[k], k)
+
+    def copy_c():
+        return remote(4, cs, cr, 0)
+
+    def no_side(d):
+        @pl.when(jnp.logical_not(has[1 - d]))
         def _():
-            for sub in range(2):
-                x_copy(sub, 1 - far).wait_send()
-            if even:
-                c_copy().wait_send()
+            xr0[d] = jnp.zeros(xr0.shape[1:], F32)
+            xr1[d] = jnp.zeros(xr1.shape[1:], F32)
+            if d == 0:
+                cr[...] = jnp.zeros(cr.shape, F32)
+
+    for d in range(2):
+        no_side(d)
+
+    def first_collide(t):
+        post = relax_delta([f[q, :, cols(t)] for q in range(19)])
+        store_post(post, pa, packs, xs0, keys[...], t, lane)
+
+    def second_collide(t, have=None):
+        cur = stream(pa, gh.at[0], gx.at[0], code, t, lane, have=have)
+        store_post(relax_delta(cur), pb, packs, xl, keys[...], t, lane)
+
+    def finish(t):
+        cur = stream(pb, gh.at[1], gx.at[1], code, t, lane)
+        wet = (code[:, cols(t)] & (1 << BIT[0])) != 0
+        for q in range(19):
+            out[q, :, cols(t)] = jnp.where(wet, cur[q], f[q, :, cols(t)])
+
+    def gather_tile(t, sub, coarse=True):
+        for d in range(4):
+            g = jnp.dot(pyz[d], split(packs[d, :, cols(t)]), preferred_element_type=F32)
+            gh[sub, d, :, cols(t)] = g + gc[sub, :, cols(t)] if d == 0 and coarse else g
+
+    def edge_stream(k):
+        t = 3 if k == 1 else 0
+        cur = stream(pa, gh.at[0], None, code, t, lane, qs=OTHERS[k])
+        for s, tile in enumerate(pack_halves(cur, k, lane)):
+            xs1[k, :, cols(s)] = tile
+        return {q: v for q, v in zip(OTHERS[k], cur) if VEL[q][0] == 0}
+
+    def local_x(d, src):
+        return jnp.dot(pxl[d], split(src[d]), preferred_element_type=F32)
+
+    def take_a(d):
+        pl.when(has[1 - d])(lambda: copy_a(d).wait_recv())
+        far = jnp.dot(pxr[d], split(xr0[d]), preferred_element_type=F32)
+        g0[d] = g0[d] + far
+        for s in range(5):
+            gx[0, d, s] = layer(g0, d, s)
+
+    def take_b(d):
+        pl.when(has[1 - d])(lambda: copy_b(d).wait_recv())
+        g1[d] = jnp.dot(pxr[d], split(xr1[d]), preferred_element_type=F32)
+        vals = far_edge(pa, d, g0, g1, ct, lane)
+        for s in range(5):
+            gx[1, d, s] = vals[s]
+
+    def join(d):
+        near = local_x(d, xl)
+        theirs = rm[d] != 0.0
+        for s in range(5):
+            tile = near[:, (s // 2) * TILE : (s // 2 + 1) * TILE]
+            tile = roll(tile, 64) if s % 2 else tile
+            gx[1, d, s] = jnp.where(theirs, gx[1, d, s], tile)
+
+    in_n.wait()
+    in_i.wait()
+    build_tables(me, nv, iv, pyz, pxl, pxr, pc, pw, rm, keys)
+    in_c.wait()
+    coarse_ghost(cfv, cs)
+    in_s.wait()
+    build_code(sv, pw, code, lane)
+    in_3.wait()
+    first_collide(3)
+    gather_tile(3, 0, coarse=False)
+    have3 = edge_stream(1)
+    for q in CROSS[2]:
+        have3.pop(q, None)
+    pl.semaphore_wait(barrier, has[0].astype(I32) + has[1].astype(I32))
+    pl.when(has[0])(lambda: copy_c().start())
+
+    @pl.when(has[1])
+    def _():
+        copy_a(1).start()
+        copy_b(1).start()
+
+    in_0.wait()
+    first_collide(0)
+    pl.when(has[0])(lambda: copy_a(0).start())
+    in_m.wait()
+    first_collide(1)
+    first_collide(2)
+    ct[...] = coarse_table(cs, 0, (3,))
+    for d in range(2):
+        g0[d] = local_x(d, xs0)
+
+    pl.when(has[1])(lambda: copy_c().wait_recv())
+    for k in range(2):
+        gc[k] = jnp.dot(pc[...], coarse_table(cr, k, range(4)), preferred_element_type=F32)
+    gather_tile(0, 0)
+    have0 = edge_stream(0)
+    pl.when(has[0])(lambda: copy_b(0).start())
+    gather_tile(1, 0)
+    gather_tile(2, 0)
+    gh[0, 0, :, cols(3)] = gh[0, 0, :, cols(3)] + gc[0, :, cols(3)]
+    second_collide(1)
+    second_collide(2)
+
+    def tail(near):
+        far = 1 - near
+        tile = {0: 3, 1: 0}
+        mid = {0: 2, 1: 1}
+        haves = {0: have3, 1: have0}
+        take_a(near)
+        second_collide(tile[near], haves[near])
+        take_b(near)
+        gather_tile(1, 1)
+        gather_tile(2, 1)
+        take_a(far)
+        second_collide(tile[far], haves[far])
+        gather_tile(3, 1)
+        gather_tile(0, 1)
+        finish(mid[near])
+        join(near)
+        finish(tile[near])
+        finish(mid[far])
+        take_b(far)
+        join(far)
+        finish(tile[far])
 
     is_even = lax.rem(me, 2) == 0
-    pl.when(is_even)(lambda: run(True))
-    pl.when(jnp.logical_not(is_even))(lambda: run(False))
+    pl.when(is_even)(lambda: tail(0))
+    pl.when(jnp.logical_not(is_even))(lambda: tail(1))
+
+    def drain(k):
+        copy_a(k).wait_send()
+        copy_b(k).wait_send()
+        if k == 0:
+            copy_c().wait_send()
+
+    both(drain)
 
 
 def body(populations, coarse_faces, neighbors, interface, solid):
@@ -565,11 +646,15 @@
             big,
             big,
             vm((4, BLK, 512), F32),
-            vm((4, BLK, 512), F32),
+            vm((2, 4, BLK, 512), F32),
+            vm((2, BLK, 384), F32),
+            vm((2, BLK, 896), F32),
+            vm((2, 2, 5, BLK, TILE), F32),
             vm((2, BLK, 384), F32),
             vm((2, BLK, 384), F32),
-            vm((2, 2, BLK, 384), F32),
-            vm((2, 2, BLK, 384), F32),
+            vm((2, BLK, 896), F32),
+            vm((2, BLK, 896), F32),
+            vm((2, BLK, 384), F32),
             vm((2, 19, 2, 64), F32),
             vm((6, BLK), I32),
             vm((2, BLK), I32),
@@ -579,10 +664,13 @@
             vm((2, BLK, 512), F32),
             vm((BLK, 512), I32),
             vm((6, BLK, TILE), I32),
+            vm((2, BLK, TILE), F32),
+            vm((BLK, TILE), F32),
             vm((4, BLK, 2 * BLK), BF16),
             vm((2, BLK, 2 * BLK), BF16),
             vm((2, BLK, 2 * BLK), BF16),
             vm((BLK, TILE), BF16),
+            vm((TILE, TILE), BF16),
             pltpu.SemaphoreType.DMA((7,)),
             pltpu.SemaphoreType.DMA((5,)),
             pltpu.SemaphoreType.DMA((5,)),

time: 19.4 us -> 14.1 us (0.73)
  the two profiles are of different devices: /device:TPU:256 before, /device:TPU:255 now
where the time goes in v3:
time: 14.1 us; the launch traced here: 14 us
  Pallas kernels  12.9 us (91%)
  local copies, waits for them, and re-layouts  1.04 us (7%)
    pallas_call x1, Pallas kernels, body(): pl.pallas_call(functools.partial(kernel, n), out_shape=jax.ShapeDtypeStru...  12.9 us
    unnamed x1, local copies, waits for them, and re-layouts  1.04 us

profile of v3, /device:TPU:255, one launch (start us, length us, event | category | flops | bytes accessed | tf_op | source)
XLA Modules:
  0.0 14.0 jit_solution(3433595124735215630)
XLA Ops:
  0.0 12.9 %shard_map.55 = f32[19,32,512]{2,1,0:T(8,128)S(1)} custom-call(f32[19,32,512]{2,1,0:T(8,128)} %bitcast.6, f32[2,19,2,64]{3,2,1,0:T(2,128)} %bitcast.7, s32[6,32]{1,0:T(8,128)} %bitcast.8, s32[2,32]{1,0:T(2,128)} %bitcast.9, s32[32,512]{1,0:T(8,128)} %solid.1), custom_call_target="tpu_custom_call" | custom-call | tf_op jit(solution)/shard_map/pallas_call | solution.py:639
  12.9 1.0 %copy.7 = f32[32,19,512]{2,0,1:T(8,128)} copy(f32[32,19,512]{2,0,1:T(8,128)S(1)} %bitcast.5) | data formatting | bytes 2490368

commit v4 on v3

--- a/solution.py
+++ b/solution.py
@@ -39,9 +39,15 @@
     [q for q in range(19) if VEL[q][d // 2] == (-1 if d % 2 == 0 else 1)] for d in range(6)
 ]
 BIT = [9 * (x + 1) + 3 * (y + 1) + (z + 1) for x, y, z in VEL]
-OTHERS = [[q for q in range(19) if q not in CROSS[1 - d]] for d in range(2)]
+OTHERS = [
+    [q for q in range(19) if q not in CROSS[1 - d] and q not in CROSS[2]]
+    + [q for q in CROSS[2] if q not in CROSS[1 - d]]
+    for d in range(2)
+]
 BLK = 32
 TILE = 128
+CHUNK = 16
+CHUNKS = [slice(r, r + CHUNK) for r in range(0, BLK, CHUNK)]
 
 
 def relax_delta(f):
@@ -149,7 +155,7 @@
 
 
 def lanes():
-    return lax.broadcasted_iota(I32, (BLK, TILE), 1)
+    return lax.broadcasted_iota(I32, (CHUNK, TILE), 1)
 
 
 def face_lanes(d, t, lane):
@@ -173,14 +179,14 @@
     return tiles
 
 
-def layer(ref, d, n):
-    tile = ref[d, :, cols(n // 2)]
+def layer(ref, d, n, rs):
+    tile = ref[d, rs, cols(n // 2)]
     return roll(tile, 64) if n % 2 else tile
 
 
-def store_post(post, ref, packs, xs, key, t, lane):
+def store_post(post, ref, packs, xs, key, t, lane, rs):
     for q in range(19):
-        ref[q, :, cols(t)] = post[q]
+        ref[q, rs, cols(t)] = post[q]
     low = lane & 7
     mid = (lane >> 3) & 7
     for d in range(2, 6):
@@ -190,25 +196,25 @@
             pos = mid if d < 4 else low
             by, at = (step, s) if d % 2 == 0 else (-step, 7 - s)
             acc = jnp.where(pos == at, roll(post[CROSS[d][s]], by), acc)
-        packs[d - 2, :, cols(t)] = acc
+        packs[d - 2, rs, cols(t)] = acc
     if t in (0, 3):
         d = 0 if t == 0 else 1
         vals = [post[q] for q in CROSS[d]] + [key]
         for s, tile in enumerate(pack_halves(vals, d, lane)):
-            xs[d, :, cols(s)] = tile
+            xs[d, rs, cols(s)] = tile
 
 
 def y_offset(d, s):
     return (56 - 8 * s) if d == 2 else (8 * s - 56)
 
 
-def stream(ref, gh, gx, code_ref, t, lane, qs=tuple(range(19)), have=None):
-    post = [ref[q, :, cols(t)] for q in range(19)]
-    code = code_ref[:, cols(t)]
+def stream(ref, gh, gx, code_ref, t, lane, rs, qs=tuple(range(19)), have=None, alone=False):
+    post = [ref[q, rs, cols(t)] for q in range(19)]
+    code = code_ref[rs, cols(t)]
     upper = lane >= 64
 
     def merged(ex, here, load, edge):
-        if ex == 0 or gx is None:
+        if ex == 0 or alone:
             return here
         near = t - ex
         other = load(near) if 0 <= near <= 3 else edge
@@ -226,11 +232,11 @@
             continue
         ex, ey, ez = VEL[q]
         edge = None
-        if gx is not None and ex != 0 and not 0 <= t - ex <= 3:
+        if not alone and not 0 <= t - ex <= 3:
             d = 0 if ex == -1 else 1
-            edge = gx[d, CROSS[d].index(q), :, :]
+            edge = gx[d, CROSS[d].index(q), rs, :]
         base = 64 * ex
-        src = merged(ex, post[q], lambda u: ref[q, :, cols(u)], edge)
+        src = merged(ex, post[q], lambda u: ref[q, rs, cols(u)], edge)
         moved = roll(src, base + 8 * ey + ez)
         for d, comp in ((2 if ey < 0 else 3, ey), (4 if ez < 0 else 5, ez)):
             if comp == 0:
@@ -240,32 +246,28 @@
                 off = y_offset(d, s) + base + ez
             else:
                 off = (7 - s) * (1 if d == 4 else -1) + base + 8 * ey
-            g = merged(ex, gh[d - 2, :, cols(t)], lambda u: gh[d - 2, :, cols(u)], None)
+            g = merged(ex, gh[d - 2, rs, cols(t)], lambda u: gh[d - 2, rs, cols(u)], None)
             moved = jnp.where(face_lanes(d, t, lane), roll(g, off), moved)
         usable = (code & (1 << BIT[q])) != 0
         out.append(jnp.where(usable, moved, post[OPP[q]]))
     return out
 
 
-def far_edge(ref, d, g0, g1, ct, lane):
+def far_edge(ref, d, g0, g1, ghosts, lane, rs):
     t = 3 if d == 0 else 0
     cur = [None] * 19
     for n, q in enumerate(OTHERS[d]):
-        cur[q] = layer(g1, d, n)
+        cur[q] = layer(g1, d, n, rs)
     for q in CROSS[1 - d]:
         ex, ey, ez = VEL[q]
-        moved = roll(ref[q, :, cols(t)], 64 + 8 * ey + ez)
-        back = layer(g0, d, CROSS[d].index(OPP[q]))
+        moved = roll(ref[q, rs, cols(t)], 64 + 8 * ey + ez)
+        back = layer(g0, d, CROSS[d].index(OPP[q]), rs)
         for f, comp in ((2 if ey < 0 else 3, ey), (4 if ez < 0 else 5, ez)):
             if comp:
                 moved = jnp.where(face_lanes(f, t, lane), back, moved)
         cur[q] = moved
     if d == 1:
-        tile = g0[d, :, cols(2)]
-        key = jnp.where(lane >= 64, roll(tile, 64), tile)
-        group = ((lane & 63) >> 3).astype(F32)
-        pick = jnp.where(key == group, 1.0, 0.0).astype(BF16)
-        ghost = jnp.dot(pick, ct[...], preferred_element_type=F32)
+        key, ghost = ghosts[0][rs], ghosts[1][rs]
         for s, q in enumerate(CROSS[2]):
             ex, ey, ez = VEL[q]
             if ex < 0:
@@ -276,6 +278,15 @@
             cur[q] = jnp.where(at, roll(ghost, y_offset(2, s) + 64 * ex + ez), cur[q])
     post = relax_delta(cur)
     return [post[q] for q in CROSS[d]]
+
+
+def their_coarse(g0, ct):
+    tile = g0[1, :, cols(2)]
+    lane = lax.broadcasted_iota(I32, (BLK, TILE), 1)
+    key = jnp.where(lane >= 64, roll(tile, 64), tile)
+    group = ((lane & 63) >> 3).astype(F32)
+    pick = jnp.where(key == group, 1.0, 0.0).astype(BF16)
+    return key, jnp.dot(pick, ct[...], preferred_element_type=F32)
 
 
 def coarse_ghost(cfv, cs):
@@ -349,13 +360,13 @@
         pw[d] = jnp.broadcast_to(jnp.where(there, -1, ~bits), (BLK, TILE))
 
 
-def build_code(sv, pw, code, lane):
+def build_code(sv, pw, code, lane, rs):
     yz = []
     for t in range(4):
-        fl = 1 - sv[:, cols(t)]
+        fl = 1 - sv[rs, cols(t)]
         wz = roll(fl, -1) | (fl << 1) | (roll(fl, 1) << 2)
         yz.append(roll(wz, -8) | (wz << 3) | (roll(wz, 8) << 6))
-    ones = jnp.full((BLK, TILE), -1, I32)
+    ones = jnp.full((CHUNK, TILE), -1, I32)
     row = lax.broadcasted_iota(I32, (8, TILE), 1)
     for t in range(4):
         static = jnp.full((8, TILE), -1, I32)
@@ -364,7 +375,7 @@
             masks = [face_lanes(2 * a + (0 if VEL[q][a] < 0 else 1), t, row) for a in axes]
             if all(m is not None for m in masks):
                 static = jnp.where(masks[0] & masks[1], static & ~(1 << BIT[q]), static)
-        static = jnp.concatenate([static] * (BLK // 8), axis=0)
+        static = jnp.concatenate([static] * (CHUNK // 8), axis=0)
         below = yz[t - 1] if t > 0 else ones
         above = yz[t + 1] if t < 3 else ones
         up = roll(jnp.where(lane >= 64, below, yz[t]), 64) << 18
@@ -373,8 +384,8 @@
         for d in range(6):
             m = face_lanes(d, t, lane)
             if m is not None:
-                word = word & jnp.where(m, pw[d], -1)
-        code[:, cols(t)] = word
+                word = word & jnp.where(m, pw[d, rs, :], -1)
+        code[rs, cols(t)] = word
 
 
 def coarse_table(src, k, tiles):
@@ -499,30 +510,47 @@
         no_side(d)
 
     def first_collide(t):
-        post = relax_delta([f[q, :, cols(t)] for q in range(19)])
-        store_post(post, pa, packs, xs0, keys[...], t, lane)
-
-    def second_collide(t, have=None):
-        cur = stream(pa, gh.at[0], gx.at[0], code, t, lane, have=have)
-        store_post(relax_delta(cur), pb, packs, xl, keys[...], t, lane)
+        for rs in CHUNKS:
+            post = relax_delta([f[q, rs, cols(t)] for q in range(19)])
+            store_post(post, pa, packs, xs0, keys[rs, :], t, lane, rs)
+
+    def second_collide(t):
+        for n, rs in enumerate(CHUNKS):
+            cur = stream(pa, gh.at[0], gx.at[0], code, t, lane, rs, have=have[t][n])
+            store_post(relax_delta(cur), pb, packs, xl, keys[rs, :], t, lane, rs)
+
+    have = [[{} for _ in CHUNKS] for _ in range(4)]
+
+    def early(t, qs):
+        for n, rs in enumerate(CHUNKS):
+            qs = [q for q in qs if q not in have[t][n]]
+            cur = stream(pa, gh.at[0], gx.at[0], code, t, lane, rs, qs=qs)
+            have[t][n].update(zip(qs, cur))
 
     def finish(t):
-        cur = stream(pb, gh.at[1], gx.at[1], code, t, lane)
-        wet = (code[:, cols(t)] & (1 << BIT[0])) != 0
-        for q in range(19):
-            out[q, :, cols(t)] = jnp.where(wet, cur[q], f[q, :, cols(t)])
+        for rs in CHUNKS:
+            cur = stream(pb, gh.at[1], gx.at[1], code, t, lane, rs)
+            wet = (code[rs, cols(t)] & (1 << BIT[0])) != 0
+            for q in range(19):
+                out[q, rs, cols(t)] = jnp.where(wet, cur[q], f[q, rs, cols(t)])
 
     def gather_tile(t, sub, coarse=True):
         for d in range(4):
             g = jnp.dot(pyz[d], split(packs[d, :, cols(t)]), preferred_element_type=F32)
             gh[sub, d, :, cols(t)] = g + gc[sub, :, cols(t)] if d == 0 and coarse else g
 
-    def edge_stream(k):
+    def edge_stream(k, part):
         t = 3 if k == 1 else 0
-        cur = stream(pa, gh.at[0], None, code, t, lane, qs=OTHERS[k])
-        for s, tile in enumerate(pack_halves(cur, k, lane)):
-            xs1[k, :, cols(s)] = tile
-        return {q: v for q, v in zip(OTHERS[k], cur) if VEL[q][0] == 0}
+        qs = OTHERS[k][part]
+        for n, rs in enumerate(CHUNKS):
+            cur = stream(
+                pa, gh.at[0], None, code, t, lane, rs, qs=qs, have=have[t][n], alone=True
+            )
+            for s, tile in enumerate(pack_halves(cur, k, lane)):
+                xs1[k, rs, cols((part.start or 0) // 2 + s)] = tile
+            for q, v in zip(qs, cur):
+                if VEL[q][0] == 0 and (k == 0 or q not in CROSS[2]):
+                    have[t][n][q] = v
 
     def local_x(d, src):
         return jnp.dot(pxl[d], split(src[d]), preferred_element_type=F32)
@@ -532,14 +560,16 @@
         far = jnp.dot(pxr[d], split(xr0[d]), preferred_element_type=F32)
         g0[d] = g0[d] + far
         for s in range(5):
-            gx[0, d, s] = layer(g0, d, s)
+            gx[0, d, s] = layer(g0, d, s, slice(None))
 
     def take_b(d):
         pl.when(has[1 - d])(lambda: copy_b(d).wait_recv())
         g1[d] = jnp.dot(pxr[d], split(xr1[d]), preferred_element_type=F32)
-        vals = far_edge(pa, d, g0, g1, ct, lane)
-        for s in range(5):
-            gx[1, d, s] = vals[s]
+        ghosts = their_coarse(g0, ct) if d == 1 else None
+        for rs in CHUNKS:
+            vals = far_edge(pa, d, g0, g1, ghosts, lane, rs)
+            for s in range(5):
+                gx[1, d, s, rs, :] = vals[s]
 
     def join(d):
         near = local_x(d, xl)
@@ -549,19 +579,21 @@
             tile = roll(tile, 64) if s % 2 else tile
             gx[1, d, s] = jnp.where(theirs, gx[1, d, s], tile)
 
+    def coarse_fine(k):
+        gc[k] = jnp.dot(pc[...], coarse_table(cr, k, range(4)), preferred_element_type=F32)
+
     in_n.wait()
     in_i.wait()
     build_tables(me, nv, iv, pyz, pxl, pxr, pc, pw, rm, keys)
     in_c.wait()
     coarse_ghost(cfv, cs)
     in_s.wait()
-    build_code(sv, pw, code, lane)
+    for rs in CHUNKS:
+        build_code(sv, pw, code, lane, rs)
     in_3.wait()
     first_collide(3)
     gather_tile(3, 0, coarse=False)
-    have3 = edge_stream(1)
-    for q in CROSS[2]:
-        have3.pop(q, None)
+    edge_stream(1, slice(None))
     pl.semaphore_wait(barrier, has[0].astype(I32) + has[1].astype(I32))
     pl.when(has[0])(lambda: copy_c().start())
 
@@ -579,31 +611,35 @@
     ct[...] = coarse_table(cs, 0, (3,))
     for d in range(2):
         g0[d] = local_x(d, xs0)
+    for t in range(3):
+        gather_tile(t, 0, coarse=False)
+    edge_stream(0, slice(0, 10))
+    dry = [q for q in range(19) if q not in CROSS[2]]
+    early(0, [q for q in dry if VEL[q][0] != 1])
+    early(1, dry)
+    early(2, dry)
+    early(3, [q for q in dry if VEL[q][0] != -1])
 
     pl.when(has[1])(lambda: copy_c().wait_recv())
-    for k in range(2):
-        gc[k] = jnp.dot(pc[...], coarse_table(cr, k, range(4)), preferred_element_type=F32)
-    gather_tile(0, 0)
-    have0 = edge_stream(0)
+    coarse_fine(0)
+    gh[0, 0] = gh[0, 0] + gc[0]
+    edge_stream(0, slice(10, 14))
     pl.when(has[0])(lambda: copy_b(0).start())
-    gather_tile(1, 0)
-    gather_tile(2, 0)
-    gh[0, 0, :, cols(3)] = gh[0, 0, :, cols(3)] + gc[0, :, cols(3)]
     second_collide(1)
     second_collide(2)
+    coarse_fine(1)
 
     def tail(near):
         far = 1 - near
         tile = {0: 3, 1: 0}
         mid = {0: 2, 1: 1}
-        haves = {0: have3, 1: have0}
         take_a(near)
-        second_collide(tile[near], haves[near])
+        second_collide(tile[near])
         take_b(near)
         gather_tile(1, 1)
         gather_tile(2, 1)
         take_a(far)
-        second_collide(tile[far], haves[far])
+        second_collide(tile[far])
         gather_tile(3, 1)
         gather_tile(0, 1)
         finish(mid[near])

time: 14.1 us -> 13.7 us (0.972)
  Pallas kernels: 12.9 us -> 12.5 us
    pallas_call x1, Pallas kernels: 12.9 us -> 12.5 us  [body(): pl.pallas_call(functools.partial(kernel, n), out_shape=jax.ShapeDtypeStru...]
where the time goes in v4:
time: 13.7 us; the launch traced here: 13.6 us
  Pallas kernels  12.5 us (91%)
  local copies, waits for them, and re-layouts  1.04 us (8%)
    pallas_call x1, Pallas kernels, body(): pl.pallas_call(functools.partial(kernel, n), out_shape=jax.ShapeDtypeStru...  12.5 us
    unnamed x1, local copies, waits for them, and re-layouts  1.04 us

profile of v4, /device:TPU:255, one launch (start us, length us, event | category | flops | bytes accessed | tf_op | source)
XLA Modules:
  0.0 13.6 jit_solution(5345140479054538694)
XLA Ops:
  0.0 12.5 %shard_map.55 = f32[19,32,512]{2,1,0:T(8,128)S(1)} custom-call(f32[19,32,512]{2,1,0:T(8,128)} %bitcast.6, f32[2,19,2,64]{3,2,1,0:T(2,128)} %bitcast.7, s32[6,32]{1,0:T(8,128)} %bitcast.8, s32[2,32]{1,0:T(2,128)} %bitcast.9, s32[32,512]{1,0:T(8,128)} %solid.1), custom_call_target="tpu_custom_call" | custom-call | tf_op jit(solution)/shard_map/pallas_call | solution.py:675
  12.5 1.0 %copy.7 = f32[32,19,512]{2,0,1:T(8,128)} copy(f32[32,19,512]{2,0,1:T(8,128)S(1)} %bitcast.5) | data formatting | bytes 2490368

commit v5 on v4

--- a/solution.py
+++ b/solution.py
@@ -187,25 +187,16 @@
 def store_post(post, ref, packs, xs, key, t, lane, rs):
     for q in range(19):
         ref[q, rs, cols(t)] = post[q]
-    low = lane & 7
-    mid = (lane >> 3) & 7
-    for d in range(2, 6):
-        acc = post[CROSS[d][0]]
-        for s in range(1, 5):
-            step = (8 if d < 4 else 1) * s
-            pos = mid if d < 4 else low
-            by, at = (step, s) if d % 2 == 0 else (-step, 7 - s)
-            acc = jnp.where(pos == at, roll(post[CROSS[d][s]], by), acc)
-        packs[d - 2, rs, cols(t)] = acc
+    first = [face_lanes(3, t, lane), face_lanes(5, t, lane)]
+    for h in range(2):
+        for n in range(5):
+            a, b = CROSS[2 + 2 * h][n], CROSS[3 + 2 * h][n]
+            packs[5 * h + n, rs, cols(t)] = jnp.where(first[h], post[a], post[b])
     if t in (0, 3):
         d = 0 if t == 0 else 1
         vals = [post[q] for q in CROSS[d]] + [key]
         for s, tile in enumerate(pack_halves(vals, d, lane)):
             xs[d, rs, cols(s)] = tile
-
-
-def y_offset(d, s):
-    return (56 - 8 * s) if d == 2 else (8 * s - 56)
 
 
 def stream(ref, gh, gx, code_ref, t, lane, rs, qs=tuple(range(19)), have=None, alone=False):
@@ -235,19 +226,25 @@
         if not alone and not 0 <= t - ex <= 3:
             d = 0 if ex == -1 else 1
             edge = gx[d, CROSS[d].index(q), rs, :]
-        base = 64 * ex
         src = merged(ex, post[q], lambda u: ref[q, rs, cols(u)], edge)
-        moved = roll(src, base + 8 * ey + ez)
-        for d, comp in ((2 if ey < 0 else 3, ey), (4 if ez < 0 else 5, ez)):
-            if comp == 0:
-                continue
-            s = CROSS[d].index(q)
-            if d < 4:
-                off = y_offset(d, s) + base + ez
-            else:
-                off = (7 - s) * (1 if d == 4 else -1) + base + 8 * ey
-            g = merged(ex, gh[d - 2, rs, cols(t)], lambda u: gh[d - 2, rs, cols(u)], None)
-            moved = jnp.where(face_lanes(d, t, lane), roll(g, off), moved)
+
+        def ghost(n, at):
+            here = gh[n, rs, cols(t)]
+            if ex == 0 or alone or not 0 <= t - ex <= 3:
+                return here
+            other = gh[n, rs, cols(t - ex)]
+            return jnp.where(at, other, here) if ex == 1 else jnp.where(at, here, other)
+
+        if ey:
+            d = 2 if ey < 0 else 3
+            g = ghost(CROSS[d].index(q), jnp.logical_not(upper))
+            src = jnp.where(face_lanes(d ^ 1, t, lane), g, src)
+        if ez:
+            d = 4 if ez < 0 else 5
+            wrapped = face_lanes(3 if ez < 0 else 2, t, lane)
+            g = ghost(5 + CROSS[d].index(q), jnp.logical_xor(upper, wrapped))
+            src = jnp.where(face_lanes(d ^ 1, t, lane), g, src)
+        moved = roll(src, 64 * ex + 8 * ey + ez)
         usable = (code & (1 << BIT[q])) != 0
         out.append(jnp.where(usable, moved, post[OPP[q]]))
     return out
@@ -267,7 +264,8 @@
                 moved = jnp.where(face_lanes(f, t, lane), back, moved)
         cur[q] = moved
     if d == 1:
-        key, ghost = ghosts[0][rs], ghosts[1][rs]
+        key = ghosts[0][rs]
+        ghost = [g[rs] for g in ghosts[1]]
         for s, q in enumerate(CROSS[2]):
             ex, ey, ez = VEL[q]
             if ex < 0:
@@ -275,7 +273,7 @@
             at = face_lanes(2, 3, lane) & (key >= 0.0)
             if ez:
                 at = at & jnp.logical_not(face_lanes(4 if ez < 0 else 5, 3, lane))
-            cur[q] = jnp.where(at, roll(ghost, y_offset(2, s) + 64 * ex + ez), cur[q])
+            cur[q] = jnp.where(at, roll(ghost[s], ez), cur[q])
     post = relax_delta(cur)
     return [post[q] for q in CROSS[d]]
 
@@ -284,9 +282,15 @@
     tile = g0[1, :, cols(2)]
     lane = lax.broadcasted_iota(I32, (BLK, TILE), 1)
     key = jnp.where(lane >= 64, roll(tile, 64), tile)
+    out = jnp.dot(coarse_pick(key, lane), ct[...], preferred_element_type=F32)
+    return key, [out[BLK * n : BLK * (n + 1)] for n in range(5)]
+
+
+def coarse_pick(key, lane):
     group = ((lane & 63) >> 3).astype(F32)
-    pick = jnp.where(key == group, 1.0, 0.0).astype(BF16)
-    return key, jnp.dot(pick, ct[...], preferred_element_type=F32)
+    mine = key == group
+    rows = [jnp.where(mine & ((lane & 7) == n), 1.0, 0.0) for n in range(5)]
+    return jnp.concatenate(rows, axis=0).astype(BF16)
 
 
 def coarse_ghost(cfv, cs):
@@ -347,11 +351,10 @@
             mine = (there >= 0.0) & (there < float(BLK))
             rm[d] = jnp.broadcast_to(jnp.where(mine, 1.0, 0.0), (BLK, TILE))
         else:
-            pyz[d - 2] = one
+            pyz[d // 2 - 1, BLK * (d % 2) : BLK * (d % 2 + 1)] = one
     key = jnp.where(cb >= 0.0, 2.0 * quad + cb - 2.0 * (me + 1).astype(F32), -1.0)
     keys[...] = jnp.broadcast_to(key, (BLK, TILE))
-    group = ((lax.broadcasted_iota(I32, (BLK, TILE), 1) & 63) >> 3).astype(F32)
-    pc[...] = jnp.where(key == group, 1.0, 0.0).astype(BF16)
+    pc[...] = coarse_pick(key, lax.broadcasted_iota(I32, (BLK, TILE), 1))
     for d in range(6):
         there = face[d] >= 0.0
         if d == 2:
@@ -389,10 +392,7 @@
 
 
 def coarse_table(src, k, tiles):
-    lane = lax.broadcasted_iota(I32, (8, TILE), 1)
-    srow = lax.broadcasted_iota(I32, (8, TILE), 0)
-    half = (lane & 7) >> 1
-    at = (lane >> 3) & 7
+    half = (lax.broadcasted_iota(I32, (8, TILE), 1) & 7) >> 1
     parts = []
     for quadrant in range(4):
         for c in range(2):
@@ -401,7 +401,7 @@
             for t in tiles:
                 idx = half + (32 * (quadrant // 2) + 4 * (quadrant % 2) + 8 * t)
                 got = jnp.take_along_axis(vals, idx, axis=1, mode="promise_in_bounds")
-                wide.append(jnp.where(at == srow, got, 0.0))
+                wide.append(got)
             parts.append(jnp.concatenate(wide, axis=1))
     return split(jnp.concatenate(parts, axis=0))
 
@@ -534,10 +534,23 @@
             for q in range(19):
                 out[q, rs, cols(t)] = jnp.where(wet, cur[q], f[q, rs, cols(t)])
 
+    whole = lax.broadcasted_iota(I32, (BLK, TILE), 1)
+
     def gather_tile(t, sub, coarse=True):
-        for d in range(4):
-            g = jnp.dot(pyz[d], split(packs[d, :, cols(t)]), preferred_element_type=F32)
-            gh[sub, d, :, cols(t)] = g + gc[sub, :, cols(t)] if d == 0 and coarse else g
+        for h in range(2):
+            src = jnp.concatenate([packs[5 * h + i, :, cols(t)] for i in range(5)], axis=1)
+            got = jnp.dot(pyz[h], split(src), preferred_element_type=F32)
+            first = face_lanes(3 + 2 * h, t, whole)
+            for i in range(5):
+                part = slice(TILE * i, TILE * (i + 1))
+                a, b = got[:BLK, part], got[BLK:, part]
+                if h == 0:
+                    if coarse:
+                        a = a + gc[sub, i, :, cols(t)]
+                    ghosts = roll(jnp.where(first, a, b), 64)
+                else:
+                    ghosts = jnp.where(first, roll(a, 8), roll(b, -8))
+                gh[sub, 5 * h + i, :, cols(t)] = ghosts
 
     def edge_stream(k, part):
         t = 3 if k == 1 else 0
@@ -580,7 +593,9 @@
             gx[1, d, s] = jnp.where(theirs, gx[1, d, s], tile)
 
     def coarse_fine(k):
-        gc[k] = jnp.dot(pc[...], coarse_table(cr, k, range(4)), preferred_element_type=F32)
+        got = jnp.dot(pc[...], coarse_table(cr, k, range(4)), preferred_element_type=F32)
+        for i in range(5):
+            gc[k, i] = got[BLK * i : BLK * (i + 1)]
 
     in_n.wait()
     in_i.wait()
@@ -622,7 +637,9 @@
 
     pl.when(has[1])(lambda: copy_c().wait_recv())
     coarse_fine(0)
-    gh[0, 0] = gh[0, 0] + gc[0]
+    first = face_lanes(3, 0, lax.broadcasted_iota(I32, (BLK, 4 * TILE), 1))
+    for i in range(5):
+        gh[0, i] = jnp.where(first, gh[0, i] + gc[0, i], gh[0, i])
     edge_stream(0, slice(10, 14))
     pl.when(has[0])(lambda: copy_b(0).start())
     second_collide(1)
@@ -681,8 +698,8 @@
             big,
             big,
             big,
-            vm((4, BLK, 512), F32),
-            vm((2, 4, BLK, 512), F32),
+            vm((10, BLK, 512), F32),
+            vm((2, 10, BLK, 512), F32),
             vm((2, BLK, 384), F32),
             vm((2, BLK, 896), F32),
             vm((2, 2, 5, BLK, TILE), F32),
@@ -697,15 +714,15 @@
             vm((BLK, 512), I32),
             vm((2, 16, TILE), F32),
             vm((2, 16, TILE), F32),
-            vm((2, BLK, 512), F32),
+            vm((2, 5, BLK, 512), F32),
             vm((BLK, 512), I32),
             vm((6, BLK, TILE), I32),
             vm((2, BLK, TILE), F32),
             vm((BLK, TILE), F32),
-            vm((4, BLK, 2 * BLK), BF16),
+            vm((2, 2 * BLK, 2 * BLK), BF16),
             vm((2, BLK, 2 * BLK), BF16),
             vm((2, BLK, 2 * BLK), BF16),
-            vm((BLK, TILE), BF16),
+            vm((5 * BLK, TILE), BF16),
             vm((TILE, TILE), BF16),
             pltpu.SemaphoreType.DMA((7,)),
             pltpu.SemaphoreType.DMA((5,)),

time: 13.7 us -> 13.6 us (level)
  no operation moved by 1% of the time
where the time goes in v5:
time: 13.6 us; the launch traced here: 13.5 us
  Pallas kernels  12.4 us (91%)
  local copies, waits for them, and re-layouts  1.04 us (8%)
    pallas_call x1, Pallas kernels, body(): pl.pallas_call(functools.partial(kernel, n), out_shape=jax.ShapeDtypeStru...  12.4 us
    unnamed x1, local copies, waits for them, and re-layouts  1.04 us

profile of v5, /device:TPU:255, one launch (start us, length us, event | category | flops | bytes accessed | tf_op | source)
XLA Modules:
  0.0 13.5 jit_solution(5545102524985120460)
XLA Ops:
  0.0 12.4 %shard_map.55 = f32[19,32,512]{2,1,0:T(8,128)S(1)} custom-call(f32[19,32,512]{2,1,0:T(8,128)} %bitcast.6, f32[2,19,2,64]{3,2,1,0:T(2,128)} %bitcast.7, s32[6,32]{1,0:T(8,128)} %bitcast.8, s32[2,32]{1,0:T(2,128)} %bitcast.9, s32[32,512]{1,0:T(8,128)} %solid.1), custom_call_target="tpu_custom_call" | custom-call | tf_op jit(solution)/shard_map/pallas_call | solution.py:692
  12.4 1.0 %copy.7 = f32[32,19,512]{2,0,1:T(8,128)} copy(f32[32,19,512]{2,0,1:T(8,128)S(1)} %bitcast.5) | data formatting | bytes 2490368

commit v6 on v5

--- a/solution.py
+++ b/solution.py
@@ -609,17 +609,15 @@
     first_collide(3)
     gather_tile(3, 0, coarse=False)
     edge_stream(1, slice(None))
-    pl.semaphore_wait(barrier, has[0].astype(I32) + has[1].astype(I32))
-    pl.when(has[0])(lambda: copy_c().start())
-
-    @pl.when(has[1])
+
+    @pl.when(me == 0)
     def _():
+        pl.semaphore_wait(barrier, 1)
         copy_a(1).start()
         copy_b(1).start()
 
     in_0.wait()
     first_collide(0)
-    pl.when(has[0])(lambda: copy_a(0).start())
     in_m.wait()
     first_collide(1)
     first_collide(2)
@@ -635,6 +633,25 @@
     early(2, dry)
     early(3, [q for q in dry if VEL[q][0] != -1])
 
+    @pl.when(me > 0)
+    def _():
+        pl.semaphore_wait(barrier, 1 + has[1].astype(I32))
+        copy_c().start()
+
+        @pl.when(has[1])
+        def _():
+            copy_a(1).start()
+            copy_b(1).start()
+
+        copy_a(0).start()
+
+    odd = lax.rem(me, 2) == 1
+
+    def take_near():
+        take_a(1)
+        take_b(1)
+
+    pl.when(odd & (me != 1))(take_near)
     pl.when(has[1])(lambda: copy_c().wait_recv())
     coarse_fine(0)
     first = face_lanes(3, 0, lax.broadcasted_iota(I32, (BLK, 4 * TILE), 1))
@@ -650,9 +667,13 @@
         far = 1 - near
         tile = {0: 3, 1: 0}
         mid = {0: 2, 1: 1}
-        take_a(near)
-        second_collide(tile[near])
-        take_b(near)
+        if near == 0:
+            take_a(near)
+            second_collide(tile[near])
+            take_b(near)
+        else:
+            pl.when(me == 1)(take_near)
+            second_collide(tile[near])
         gather_tile(1, 1)
         gather_tile(2, 1)
         take_a(far)
@@ -667,9 +688,8 @@
         join(far)
         finish(tile[far])
 
-    is_even = lax.rem(me, 2) == 0
-    pl.when(is_even)(lambda: tail(0))
-    pl.when(jnp.logical_not(is_even))(lambda: tail(1))
+    pl.when(jnp.logical_not(odd))(lambda: tail(0))
+    pl.when(odd)(lambda: tail(1))
 
     def drain(k):
         copy_a(k).wait_send()

time: 13.6 us -> 13.7 us (level)
  the two profiles are of different devices: /device:TPU:255 before, /device:TPU:1 now
where the time goes in v6:
time: 13.7 us; the launch traced here: 13.5 us
  Pallas kernels  12.5 us (91%)
  local copies, waits for them, and re-layouts  1.04 us (8%)
    pallas_call x1, Pallas kernels, body(): pl.pallas_call(functools.partial(kernel, n), out_shape=jax.ShapeDtypeStru...  12.5 us
    unnamed x1, local copies, waits for them, and re-layouts  1.04 us

profile of v6, /device:TPU:1, one launch (start us, length us, event | category | flops | bytes accessed | tf_op | source)
XLA Modules:
  0.0 13.5 jit_solution(4713298431817369194)
XLA Ops:
  0.0 12.5 %shard_map.55 = f32[19,32,512]{2,1,0:T(8,128)S(1)} custom-call(f32[19,32,512]{2,1,0:T(8,128)} %bitcast.6, f32[2,19,2,64]{3,2,1,0:T(2,128)} %bitcast.7, s32[6,32]{1,0:T(8,128)} %bitcast.8, s32[2,32]{1,0:T(2,128)} %bitcast.9, s32[32,512]{1,0:T(8,128)} %solid.1), custom_call_target="tpu_custom_call" | custom-call | tf_op jit(solution)/shard_map/pallas_call | solution.py:712
  12.5 1.0 %copy.7 = f32[32,19,512]{2,0,1:T(8,128)} copy(f32[32,19,512]{2,0,1:T(8,128)S(1)} %bitcast.5) | data formatting | bytes 2490368
